TPU v7x, 512 devices: a whole 4x4x16 slice. The times are simulated.
512 devices in a mesh: seq: 64 (over z, y), tp: 8 (over x, core).
Axes of the slice: x: 4, y: 4, z: 16, core: 2. Of those that a mesh axis runs over, the one named last changes fastest.
Arguments:
- tokens: bfloat16 [32768, 2048], P('seq', 'tp'), may hold values from -6 to 6
- in_weight: bfloat16 [2048, 2, 2048], P(None, None, 'tp'), may hold values from -0.125 to 0.125
- bc_weight: bfloat16 [2048, 256], P(None, 'tp'), may hold values from -0.125 to 0.125
- dt_weight: bfloat16 [2, 2048, 32], P(None, None, 'tp'), may hold values from -0.125 to 0.125
- dt_bias: float32 [2, 32], P(None, 'tp'), may hold values from -2 to 0.5
- decay_rate: float32 [32], P('tp'), may hold values from 1e-05 to 0.5
- skip_gain: float32 [32], P('tp'), may hold values from 0.5 to 300
- out_weight: bfloat16 [2048, 2048], P('tp'), may hold values from -0.1875 to 0.1875
Outputs:
- mixed: bfloat16 [32768, 2048], P('seq', 'tp')
All inputs are finite; a program needn't handle non-finite values.
Results may differ from a plain program's by a relative error of at most 0.018.
Values may be sent and summed in bfloat16 or wider, within the bound.
No kernel may reach another device: no remote copies, remote signals or barrier semaphores. Data moves between devices by JAX's collectives and lax.ppermute only.
A program may use at most 64 MiB of HBM per device.

v0:
```python
import jax
import jax.numpy as jnp
from jax import lax
from jax.sharding import PartitionSpec as P

HEAD_DIM = 64
STATE = 128


def carried_in(value, axis, join, neutral, backward):
    count, mine = (lax.axis_size(axis), lax.axis_index(axis))
    pieces = jax.tree.map(lambda part: lax.all_gather(part, axis), value)
    if backward:
        pieces = jax.tree.map(lambda part: part[::-1], pieces)
        mine = count - 1 - mine
    so_far = jax.tree.map(
        lambda part, zero: jnp.full_like(part, 0) + jnp.asarray(zero, part.dtype), value, neutral
    )

    def lap(position, so_far):
        longer = join(so_far, jax.tree.map(lambda part: part[position], pieces))
        return jax.tree.map(lambda new, old: jnp.where(position < mine, new, old), longer, so_far)

    return lax.fori_loop(0, count - 1, lap, so_far)


def combine_states(earlier, later):
    return (earlier[0] + later[0], jnp.exp(later[0])[:, None, None] * earlier[1] + later[1])


def shards(tokens, in_weight, bc_weight, dt_weight, dt_bias, decay_rate, skip_gain, out_weight):
    whole = lax.all_gather(tokens, "tp", axis=1, tiled=True)
    length = whole.shape[0]
    heads_here = decay_rate.shape[0]
    projected = jnp.einsum("td,dkf->tkf", whole, in_weight, preferred_element_type=jnp.float32)
    values = projected[:, 0].astype(jnp.bfloat16).reshape(length, heads_here, HEAD_DIM)
    gates = projected[:, 1].reshape(length, heads_here, HEAD_DIM)
    full_columns = lax.all_gather(bc_weight, "tp", axis=1, tiled=True)
    both = jnp.dot(whole, full_columns, preferred_element_type=jnp.float32).astype(jnp.bfloat16)
    keys = both[:, :STATE]
    queries = both[:, STATE:]
    steps = jax.nn.softplus(
        jnp.einsum("td,kdh->kth", whole, dt_weight, preferred_element_type=jnp.float32)
        + dt_bias[:, None, :]
    )
    forward_steps = steps[0]
    backward_steps = steps[1]
    forward_logs = -decay_rate[None, :] * forward_steps
    backward_logs = -decay_rate[None, :] * backward_steps
    rows = jnp.arange(length, dtype=jnp.int32)[:, None]
    cols = jnp.arange(length, dtype=jnp.int32)[None, :]
    running = (rows >= cols).astype(jnp.float32)
    both_logs = jnp.concatenate([forward_logs, backward_logs], axis=1)
    both_upto = jnp.dot(
        running, both_logs, precision=lax.Precision.HIGHEST, preferred_element_type=jnp.float32
    )
    forward_upto = both_upto[:, :heads_here]
    backward_upto = both_upto[:, heads_here:]
    forward_before = forward_upto - forward_logs
    backward_before = backward_upto - backward_logs
    forward_total = forward_upto[-1]
    backward_total = backward_upto[-1]
    keys_wide = keys.astype(jnp.float32)
    forward_keys = (
        keys_wide[:, None, :]
        * (jnp.exp(forward_total[None, :] - forward_upto) * forward_steps)[:, :, None]
    ).astype(jnp.bfloat16)
    backward_keys = (
        keys_wide[:, None, :] * (jnp.exp(backward_before) * backward_steps)[:, :, None]
    ).astype(jnp.bfloat16)
    forward_state = jnp.einsum(
        "shp,shn->hpn", values, forward_keys, preferred_element_type=jnp.float32
    )
    backward_state = jnp.einsum(
        "shp,shn->hpn", values, backward_keys, preferred_element_type=jnp.float32
    )
    empty = (jnp.zeros_like(forward_total), jnp.zeros_like(forward_state))
    forward_enter = carried_in((forward_total, forward_state), "seq", combine_states, empty, False)[
        1
    ]
    backward_enter = carried_in(
        (backward_total, backward_state), "seq", combine_states, empty, True
    )[1]
    scores = lax.dot_general(
        queries, keys, (((1,), (1,)), ((), ())), preferred_element_type=jnp.float32
    )
    lower_mask = (rows > cols)[None]
    upper_mask = (rows < cols)[None]
    forward_gap = jnp.where(
        lower_mask, forward_before.T[:, :, None] - forward_upto.T[:, None, :], 0.0
    )
    forward_weights = jnp.where(
        lower_mask, scores[None] * jnp.exp(forward_gap) * forward_steps.T[:, None, :], 0.0
    ).astype(jnp.bfloat16)
    backward_gap = jnp.where(
        upper_mask, backward_before.T[:, None, :] - backward_upto.T[:, :, None], 0.0
    )
    backward_weights = jnp.where(
        upper_mask, scores[None] * jnp.exp(backward_gap) * backward_steps.T[:, None, :], 0.0
    ).astype(jnp.bfloat16)
    inner = jnp.einsum("hts,shp->thp", forward_weights, values, preferred_element_type=jnp.float32)
    inner = inner + jnp.einsum(
        "hts,shp->thp", backward_weights, values, preferred_element_type=jnp.float32
    )
    queries_wide = queries.astype(jnp.float32)
    mix = inner + jnp.exp(forward_before)[:, :, None] * jnp.einsum(
        "tn,hpn->thp", queries_wide, forward_enter, precision=lax.Precision.HIGHEST
    )
    mix = mix + jnp.exp(backward_total[None, :] - backward_upto)[:, :, None] * jnp.einsum(
        "tn,hpn->thp", queries_wide, backward_enter, precision=lax.Precision.HIGHEST
    )
    mix = mix + skip_gain[None, :, None] * values.astype(jnp.float32)
    gated = mix * jax.nn.silu(gates)
    power = jnp.mean(gated * gated, axis=-1, keepdims=True)
    hidden = (
        (gated * lax.rsqrt(power + 1e-05))
        .astype(jnp.bfloat16)
        .reshape(length, heads_here * HEAD_DIM)
    )
    partial_terms = jnp.dot(hidden, out_weight, preferred_element_type=jnp.float32)
    return lax.psum_scatter(
        partial_terms.astype(jnp.bfloat16), "tp", scatter_dimension=1, tiled=True
    )


def solution(mesh):
    in_specs = (
        P("seq", "tp"),
        P(None, None, "tp"),
        P(None, "tp"),
        P(None, None, "tp"),
        P(None, "tp"),
        P("tp"),
        P("tp"),
        P("tp", None),
    )
    out_specs = P("seq", "tp")
    return jax.shard_map(shards, mesh=mesh, in_specs=in_specs, out_specs=out_specs, check_vma=False)
```

profile of v0, /device:TPU:1, one launch (start us, length us, event | category | flops | bytes accessed | tf_op | source)
XLA Modules:
  0.0 521.8 jit_solution(10371247447169078333)
XLA Ops:
  8.7 41.4 %all-gather.9.cloned.1.call-done = bf16[512,2048]{1,0:T(8,128)(2,1)} async-done(((bf16[512,256]{1,0:T(8,128)(2,1)}), bf16[512,2048]{1,0:T(8,128)(2,1)}) %all-gather.9.cloned.1.call-update) | async-done | bytes 2097168 | tf_op jit(solution)/shard_map/all_gather | solution.py:32
  50.1 2.3 compare_select_fusion
  53.2 31.4 %all-gather.11.cloned.1.call-done = bf16[2048,256]{0,1:T(8,128)(2,1)} async-done(((bf16[2048,32]{0,1:T(8,128)(2,1)}), bf16[2048,256]{0,1:T(8,128)(2,1)}) %all-gather.11.cloned.1.call-update) | async-done | bytes 1048592 | tf_op jit(solution)/shard_map/all_gather | solution.py:38
  84.6 2.7 convolution_convert_fusion.1
  87.4 1.3 fusion.4
  89.8 1.1 fusion.24
  92.6 66.3 %all-gather.3 = f32[64,1,4]{2,1,0:T(1,128)S(1)} all-gather(f32[1,1,4]{2,1,0:T(1,128)S(1)} %bitcast.96), channel_id=1, replica_groups=mesh['seq'=64,'tp'=8] {'seq'}, dimensions={0}, use_global_device_ids=true | all-gather | bytes 1040 | tf_op jit(solution)/shard_map/all_gather | solution.py:12
  158.9 61.3 %all-gather.2 = f32[64,1,4]{2,1,0:T(1,128)S(1)} all-gather(f32[1,1,4]{2,1,0:T(1,128)S(1)} %bitcast.95), channel_id=1, replica_groups=mesh['seq'=64,'tp'=8] {'seq'}, dimensions={0}, use_global_device_ids=true | all-gather | bytes 1040 | tf_op jit(solution)/shard_map/all_gather | solution.py:12
  220.2 1.1 fusion.25
  221.3 1.3 fusion.32
  222.7 2.9 fusion.7
  225.6 2.4 fusion.16
  228.1 11.8 %all-gather.13.cloned.1.call-done = f32[256,64,128]{2,1,0:T(8,128)} async-done(((f32[4,64,128]{2,1,0:T(8,128)}), f32[256,64,128]{2,1,0:T(8,128)}) %all-gather.13.cloned.1.call-update) | async-done | bytes 8388624 | tf_op jit(solution)/shard_map/all_gather | solution.py:12
  239.8 65.5 %while.28 = (s32[]{:T(128)}, f32[4,64,128]{2,1,0:T(8,128)S(1)}, s32[]{:T(128)}, f32[64,4]{1,0:T(8,128)S(1)}, f32[64,4,64,128]{3,2,1,0:T(8,128)}, /*index=5*/s32[]{:T(128)}, s32[]{:T(128)}) while((s32[]{:T(128)}, f32[4,64,128]{2,1,0:T(8,128)S(1)}, s32[]{:T(128)}, f32[64,4]{1,0:T(8,128)S(1)}, f32[64,4,64,128]{3,2,1,0:T(8,128)}, ...), condition=%wide.region_1.2_spmd.clone, body=%wide.region_0.1_spmd.clone.sunk | while | flops 131076 | bytes 393377 | solution.py:24
  261.7 1.0 fusion.61
  265.8 1.0 fusion.61
  271.0 1.0 fusion.61
  277.3 1.0 fusion.61
  279.4 1.0 fusion.61
  280.4 1.0 fusion.61
  283.5 1.0 fusion.61
  286.6 1.0 fusion.61
  291.8 1.0 fusion.61
  295.0 1.0 fusion.61
  301.2 1.0 fusion.61
  305.3 89.6 %all-gather.15.cloned.1.call-done = f32[256,64,128]{2,1,0:T(8,128)} async-done(((f32[4,64,128]{2,1,0:T(8,128)}), f32[256,64,128]{2,1,0:T(8,128)}) %all-gather.15.cloned.1.call-update) | async-done | bytes 8388624 | tf_op jit(solution)/shard_map/all_gather | solution.py:12
  395.0 8.3 %rev.7 = f32[64,4,64,128]{3,2,1,0:T(8,128)} reverse(f32[64,4,64,128]{3,2,1,0:T(8,128)} %bitcast.84), dimensions={0} | reverse | bytes 16777216 | tf_op jit(solution)/shard_map/rev | solution.py:14
  403.3 65.6 %while.29 = (s32[]{:T(128)}, f32[4,64,128]{2,1,0:T(8,128)S(1)}, s32[]{:T(128)}, f32[64,4]{1,0:T(8,128)S(1)}, f32[64,4,64,128]{3,2,1,0:T(8,128)}, /*index=5*/s32[]{:T(128)}, s32[]{:T(128)}) while((s32[]{:T(128)}, f32[4,64,128]{2,1,0:T(8,128)S(1)}, s32[]{:T(128)}, f32[64,4]{1,0:T(8,128)S(1)}, f32[64,4,64,128]{3,2,1,0:T(8,128)}, ...), condition=%wide.region_3.4_spmd.clone, body=%wide.region_2.3_spmd.clone.sunk | while | flops 131076 | bytes 393377 | solution.py:24
  404.3 1.0 fusion.62
  405.4 1.0 fusion.62
  406.4 1.0 fusion.62
  407.5 1.0 fusion.62
  408.5 1.0 fusion.62
  409.5 1.0 fusion.62
  410.6 1.0 fusion.62
  411.6 1.0 fusion.62
  412.7 1.0 fusion.62
  415.8 1.0 fusion.62
  416.8 1.0 fusion.62
  417.9 1.0 fusion.62
  418.9 1.0 fusion.62
  420.0 1.0 fusion.62
  421.0 1.0 fusion.62
  422.0 1.0 fusion.62
  423.1 1.0 fusion.62
  435.6 1.0 fusion.62
  436.6 1.0 fusion.62
  437.7 1.0 fusion.62
  438.7 1.0 fusion.62
  439.8 1.0 fusion.62
  440.8 1.0 fusion.62
  441.8 1.0 fusion.62
  442.9 1.0 fusion.62
  455.4 1.0 fusion.62
  456.4 1.0 fusion.62
  457.5 1.0 fusion.62
  458.5 1.0 fusion.62
  459.5 1.0 fusion.62
  460.6 1.0 fusion.62
  461.6 1.0 fusion.62
  462.7 1.0 fusion.62
  469.3 1.6 multiply_reduce_fusion
  471.0 2.1 convolution_convert_fusion
  473.1 42.1 %reduce-scatter.2.cloned.1.call-done = bf16[512,256]{1,0:T(8,128)(2,1)} async-done(((bf16[512,2048]{1,0:T(8,128)(2,1)}), bf16[512,256]{1,0:T(8,128)(2,1)}) %reduce-scatter.2.cloned.1.call-update) | async-done | bytes 262160 | tf_op jit(solution)/shard_map/reduce_scatter | solution.py:121
  (250 shorter events, 89.3 us)
Async XLA Ops:
  6.5 80.8 %copy-start = (bf16[2048,2,256]{2,1,0:T(2,128)(2,1)S(1)}, bf16[2048,2,256]{2,1,0:T(2,128)(2,1)}, u32[]{:S(2)}) copy-start(bf16[2048,2,256]{2,1,0:T(2,128)(2,1)} %param.13) | copy-start | bytes 6291460
  6.5 43.6 %all-gather.9.cloned.1.call-start = ((), (), s32[]{:S(2)}) async-start(), calls=%async_computation.1 | async-start | bytes 2359296 | tf_op jit(solution)/shard_map/all_gather | solution.py:32
  7.3 77.3 %all-gather.11.cloned.1.call-start = ((), (), s32[]{:S(2)}) async-start(), calls=%async_computation.2 | async-start | bytes 1179648 | tf_op jit(solution)/shard_map/all_gather | solution.py:38
  8.0 231.8 %all-gather.13.cloned.1.call-start = ((), (), s32[]{:S(2)}) async-start(), calls=%async_computation.4 | async-start | bytes 8519680 | tf_op jit(solution)/shard_map/all_gather | solution.py:12
  84.6 2.8 copy-start.1
  88.7 1.0 copy-start.4
  91.0 304.0 %all-gather.15.cloned.1.call-start = ((), (), s32[]{:S(2)}) async-start(), calls=%async_computation.5 | async-start | bytes 8519680 | tf_op jit(solution)/shard_map/all_gather | solution.py:12
  222.6 292.6 %reduce-scatter.2.cloned.1.call-start = ((), (), s32[]{:S(2)}) async-start(), calls=%async_computation.3 | async-start | bytes 2359296 | tf_op jit(solution)/shard_map/reduce_scatter | solution.py:121
  222.7 2.9 copy-start.2
  222.7 2.9 copy-start.5
  394.9 74.3 %slice-start = ((f32[512,2,256]{0,2,1:T(8,128)}), f32[512,1,256]{0,2,1:T(8,128)S(1)}, s32[]{:S(2)}) async-start(f32[512,2,256]{0,2,1:T(8,128)} %copy-done.4), calls=%async_computation.6 | async-start | bytes 1048576 | tf_op jit(solution)/shard_map/slice | solution.py:37
  394.9 74.3 %copy-start.6 = (f32[4]{0:T(128)S(1)}, f32[4]{0:T(128)}, u32[]{:S(2)}) copy-start(f32[4]{0:T(128)} %param.18) | copy-start | bytes 52
  468.9 2.1 copy-start.3
Sparse Core Ops, SparseCore 0:
  9.5 40.6 all-gather.8
  52.3 32.2 all-gather.10
  91.1 148.7 all-gather.12
  242.6 152.2 all-gather.14
  473.3 41.9 reduce-scatter.1
where the time goes:
time: 525 us; the launch traced here: 522 us
  waiting for transfers between devices  218 us (42%)
  other arithmetic  128 us (24%)
  blocking collectives  128 us (24%)
  matrix products  19.7 us (4%)
  between operations  13.3 us (3%)
  local copies, waits for them, and re-layouts  11.1 us (2%)
    all_gather x2, blocking collectives, carried_in(): pieces = jax.tree.map(lambda part: lax.all_gather(part, axis), value)  128 us
    select_n x126, other arithmetic, lap(): jnp.where(position < mine, new, old)  126 us
    all_gather x2, waiting for transfers between devices, carried_in(): pieces = jax.tree.map(lambda part: lax.all_gather(part, axis), value)  101 us
    reduce_scatter x1, waiting for transfers between devices, shards(): lax.psum_scatter(partial_terms.astype(jnp.bfloat16), 'tp', scatter_dimens...  42.1 us
    all_gather x1, waiting for transfers between devices, shards(): whole = lax.all_gather(tokens, 'tp', axis=1, tiled=True)  41.4 us
    all_gather x1, waiting for transfers between devices, shards(): full_columns = lax.all_gather(bc_weight, 'tp', axis=1, tiled=True)  31.4 us
  transfers between devices with their start and end apart: 5, of which 5 were waited for; matrix products, arithmetic and copies ran while one was open for 15% of the time, Pallas kernels for 0%

commit v1 on v0

v1 whole, which is shorter than its diff:
```python
import jax
import jax.numpy as jnp
from jax import lax
from jax.experimental import pallas as pl
from jax.experimental.pallas import tpu as pltpu
from jax.sharding import PartitionSpec as P

F32 = jnp.float32
BF16 = jnp.bfloat16
L = 512
D = 2048
W = 256
H = 4
HD = 64
N = 128
XS = 4
GROUP = 8
SLICE = N // GROUP

X_GROUPS = [[2 * x + c for x in range(XS)] for c in range(2)]
SWAP = [(i, i ^ 1) for i in range(8)]
NEAR = [[GROUP * g + j for j in range(GROUP)] for g in range(8)]
FAR = [[GROUP * g + j for g in range(8)] for j in range(GROUP)]

VMEM = pl.BlockSpec(memory_space=pltpu.VMEM)
SMEM = pl.BlockSpec(memory_space=pltpu.SMEM)
NN = (((1,), (0,)), ((), ()))
NT = (((1,), (1,)), ((), ()))


def dot(a, b, dims=NN):
    return lax.dot_general(a, b, dims, preferred_element_type=F32)


def iota(shape, axis):
    return lax.broadcasted_iota(jnp.int32, shape, axis)


def spread(width, base, copies):
    row = iota((N, width), 0)
    want = iota((N, width), 1) // HD + base
    hit = row == want
    for q in range(1, copies):
        hit = hit | (row == want + 8 * q)
    return hit.astype(BF16)


def widen(cols, base, width):
    pick = spread(width, base, 1)
    high = cols.astype(BF16)
    low = (cols - high.astype(F32)).astype(BF16)
    return dot(high, pick) + dot(low, pick)


def column(ref, rows):
    index = iota((2 * H, 1), 0)
    out = jnp.zeros((2 * H, 1), F32)
    for i in range(2 * H):
        out = jnp.where(index == i, rows(ref, i), out)
    return out


def project_kernel(
    core_ref, bias_ref, rate_ref, a_ref, b_ref, w_ref, d_ref,
    values_ref, gates_ref, query_ref, key_ref, rows_ref, cols_ref, message_ref,
):
    c = core_ref[0]
    tokens = []
    weights = []
    steps_weights = []
    bc_weights = []
    for x in range(XS):
        for ref, j in ((a_ref, 2 * x + c), (b_ref, 2 * x + 1 - c)):
            at = pl.multiple_of(j * W, W)
            tokens.append(ref[x, 0:L, :])
            weights.append(w_ref[pl.ds(at, W), :])
            steps_weights.append(d_ref[:, pl.ds(at, W)])
            row = pl.multiple_of(L + j * 32, 32)
            bc_weights.append(
                jnp.concatenate([r[y, pl.ds(row, 32), :] for y in range(XS) for r in (a_ref, b_ref)], axis=0)
            )
    whole = jnp.concatenate(tokens, axis=1)
    bc_weight = jnp.concatenate(bc_weights, axis=1)
    narrow = jnp.concatenate([bc_weight[:N], jnp.concatenate(steps_weights, axis=1)], axis=0)
    keys_steps = dot(narrow, whole, NT)
    key = keys_steps[:N].astype(BF16)
    key_ref[...] = key
    query_ref[...] = dot(whole, bc_weight[N:], NT).astype(BF16)
    both = dot(whole, jnp.concatenate(weights, axis=0))
    values = both[:, :W].astype(BF16)
    values_ref[...] = values
    gates_ref[...] = both[:, W:]

    raw = keys_steps[N : N + 2 * H] + column(bias_ref, lambda r, i: r[i // H, i % H])
    steps = jnp.maximum(raw, 0.0) + jnp.log1p(jnp.exp(-jnp.abs(raw)))
    logs = -column(rate_ref, lambda r, i: r[i % H]) * steps
    p1 = logs.astype(BF16)
    rest = logs - p1.astype(F32)
    p2 = rest.astype(BF16)
    p3 = (rest - p2.astype(F32)).astype(BF16)
    running = (iota((L, L), 0) <= iota((L, L), 1)).astype(BF16)
    parts = jnp.concatenate([p1.astype(F32), p2.astype(F32), p3.astype(F32), jnp.zeros((8, L), F32)], axis=0)
    summed = dot(parts.astype(BF16), running)
    upto = summed[0:8] + summed[8:16] + summed[16:24]
    before = upto - logs
    total = upto[:, L - 1 : L]
    forward = iota((2 * H, L), 0) < H
    scale = jnp.exp(jnp.where(forward, total - upto, before)) * steps
    reach = jnp.exp(jnp.where(forward, before, total - upto))
    rows = jnp.concatenate(
        [upto, upto, before, steps, scale, reach, jnp.zeros((N - 48, L), F32)], axis=0
    )
    rows_ref[...] = rows[0:48]
    cols = rows.T
    cols_ref[...] = cols

    wide = values.astype(F32)
    scaled = (jnp.concatenate([wide, wide], axis=1) * widen(cols, 32, 2 * W)).astype(BF16)
    state = dot(key, scaled).astype(BF16)
    last = cols[L - 1 : L, :]
    lane = iota((1, N), 1)
    high = last.astype(BF16).astype(F32)
    extra = jnp.where(lane < 8, high, jnp.where(lane < 16, last - high, 0.0))
    extra = jnp.broadcast_to(extra, (SLICE, N)).astype(BF16)
    for k in range(GROUP):
        message_ref[k, :, 0 : 2 * W] = state[SLICE * k : SLICE * (k + 1)]
        message_ref[k, :, 2 * W : 2 * W + N] = extra


def inner_kernel(skip_ref, query_ref, key_ref, values_ref, rows_ref, cols_ref, inner_ref):
    key = key_ref[...]
    values = values_ref[...]
    tile = 128
    lane = iota((tile, W), 1) // HD

    def body(i, carry):
        at = pl.ds(pl.multiple_of(i * tile, tile), tile)
        scores = dot(query_ref[at, :], key)
        t = iota((tile, L), 0) + i * tile
        s = iota((tile, L), 1)
        lower = s < t
        upper = s > t
        own = values_ref[at, :].astype(F32)
        gain = jnp.zeros((tile, W), F32)
        out = jnp.zeros((tile, W), F32)
        for h in range(H):
            gap = jnp.where(
                lower,
                cols_ref[at, 16 + h : 17 + h] - rows_ref[h : h + 1, :],
                rows_ref[20 + h : 21 + h, :] - cols_ref[at, H + h : H + h + 1],
            )
            step = jnp.where(lower, rows_ref[24 + h : 25 + h, :], rows_ref[28 + h : 29 + h, :])
            weight = jnp.where(lower | upper, scores * jnp.exp(gap) * step, 0.0).astype(BF16)
            out = jnp.where(lane == h, dot(weight, values), out)
            gain = jnp.where(lane == h, skip_ref[h], gain)
        inner_ref[at, :] = out + gain * own
        return carry

    lax.fori_loop(0, L // tile, body, 0)


def near_states(got_ref):
    extra = got_ref[:, :, 2 * W : 2 * W + N].reshape(GROUP * SLICE, N)
    decay = jnp.exp(dot(extra, spread(2 * W, 0, 2)))
    states = [got_ref[j, :, 0 : 2 * W].astype(F32) for j in range(GROUP)]
    decays = [decay[SLICE * j : SLICE * (j + 1)] for j in range(GROUP)]
    return states, decays


def totals_kernel(group_ref, got_ref, out_ref):
    g = group_ref[0]
    states, decays = near_states(got_ref)
    forward = states[0][:, :W]
    for j in range(1, GROUP):
        forward = decays[j][:, :W] * forward + states[j][:, :W]
    backward = states[GROUP - 1][:, W:]
    for j in range(GROUP - 2, -1, -1):
        backward = decays[j][:, W:] * backward + states[j][:, W:]
    log = jnp.zeros((SLICE, N), F32)
    for j in range(GROUP):
        log = log + got_ref[j, :, 2 * W : 2 * W + N].astype(F32)
    high = log.astype(BF16).astype(F32)
    log = (high + pltpu.roll(log - high, 16, 1)).astype(BF16)
    forward = forward.astype(BF16)
    backward = backward.astype(BF16)
    for q in range(8):
        out_ref[q, :, 0:W] = jnp.where(q > g, forward, backward)
        out_ref[q, :, W : W + N] = log


def enter_kernel(group_ref, got_ref, far_ref, out_ref):
    g = group_ref[0]
    states, decays = near_states(got_ref)
    extra = far_ref[:, :, W : W + N].reshape(8 * SLICE, N)
    decay = jnp.exp(dot(extra, spread(2 * W, 0, 4)))
    forward = jnp.zeros((SLICE, W), F32)
    backward = jnp.zeros((SLICE, W), F32)
    for q in range(8):
        rows = slice(SLICE * q, SLICE * (q + 1))
        forward = jnp.where(q < g, decay[rows, :W] * forward + far_ref[q, :, 0:W].astype(F32), forward)
    for q in range(7, -1, -1):
        rows = slice(SLICE * q, SLICE * (q + 1))
        backward = jnp.where(q > g, decay[rows, W:] * backward + far_ref[q, :, 0:W].astype(F32), backward)
    for j in range(GROUP):
        out_ref[j, :, 0:W] = forward.astype(BF16)
        forward = decays[j][:, :W] * forward + states[j][:, :W]
    for j in range(GROUP - 1, -1, -1):
        out_ref[j, :, W : 2 * W] = backward.astype(BF16)
        backward = decays[j][:, W:] * backward + states[j][:, W:]


def mix_kernel(core_ref, inner_ref, gates_ref, query_ref, enter_ref, cols_ref, w_ref, hidden_ref, part_ref):
    carried = dot(query_ref[...], enter_ref[...]) * widen(cols_ref[...], 40, 2 * W)
    mix = inner_ref[...] + carried[:, :W] + carried[:, W:]
    gates = gates_ref[...]
    gated = mix * (gates / (1.0 + jnp.exp(-gates)))
    square = gated * gated
    same = (iota((W, W), 0) // HD == iota((W, W), 1) // HD).astype(BF16)
    high = square.astype(BF16)
    low = (square - high.astype(F32)).astype(BF16)
    power = (dot(high, same) + dot(low, same)) * (1.0 / HD)
    hidden = (gated * lax.rsqrt(power + 1e-05)).astype(BF16)
    hidden_ref[...] = hidden
    other = 1 - core_ref[0]
    for x in range(XS):
        at = pl.multiple_of((2 * x + other) * W, W)
        part_ref[x] = dot(hidden, w_ref[:, pl.ds(at, W)]).astype(BF16)


def pair_kernel(core_ref, hidden_ref, w_ref, got_ref, out_ref):
    hidden = hidden_ref[...]
    for x in range(XS):
        at = pl.multiple_of((2 * x + core_ref[0]) * W, W)
        out_ref[x] = (dot(hidden, w_ref[:, pl.ds(at, W)]) + got_ref[x].astype(F32)).astype(BF16)


def call(kernel, name, ins, outs, flops, *operands):
    return pl.pallas_call(
        kernel,
        name=name,
        in_specs=ins,
        out_specs=[VMEM] * len(outs),
        out_shape=[jax.ShapeDtypeStruct(shape, kind) for shape, kind in outs],
        compiler_params=pltpu.CompilerParams(vmem_limit_bytes=48 << 20),
        cost_estimate=pl.CostEstimate(flops=flops, bytes_accessed=1 << 21, transcendentals=1 << 16),
    )(*operands)


def shards(tokens, in_weight, bc_weight, dt_weight, dt_bias, decay_rate, skip_gain, out_weight):
    core = (lax.axis_index("tp") % 2).astype(jnp.int32)[None]
    group = (lax.axis_index("seq") // GROUP).astype(jnp.int32)[None]
    bc_rows = bc_weight.T.reshape(32, 8, W).transpose(1, 0, 2).reshape(8 * 32, W)
    payload = jnp.concatenate([tokens, bc_rows], axis=0)
    payload = jnp.broadcast_to(payload[None], (XS, L + W, W))
    mine = lax.all_to_all(payload, "tp", 0, 0, axis_index_groups=X_GROUPS, tiled=True)
    theirs = lax.ppermute(mine, "tp", SWAP)
    flat_weight = in_weight.reshape(D, 2 * W)
    steps_weight = jnp.pad(dt_weight.transpose(0, 2, 1).reshape(2 * H, D), ((0, 8), (0, 0)))
    values, gates, query, key, rows, cols, message = call(
        project_kernel,
        "project",
        [SMEM, SMEM, SMEM, VMEM, VMEM, VMEM, VMEM],
        [
            ((L, W), BF16),
            ((L, W), F32),
            ((L, N), BF16),
            ((N, L), BF16),
            ((48, L), F32),
            ((L, N), F32),
            ((GROUP, SLICE, 2 * W + N), BF16),
        ],
        1 << 31,
        core, dt_bias, decay_rate, mine, theirs, flat_weight, steps_weight,
    )
    near = lax.all_to_all(message, "seq", 0, 0, axis_index_groups=NEAR, tiled=True)
    (inner,) = call(
        inner_kernel,
        "inside",
        [SMEM, VMEM, VMEM, VMEM, VMEM, VMEM],
        [((L, W), F32)],
        1 << 31,
        skip_gain, query, key, values, rows, cols,
    )
    (totals,) = call(
        totals_kernel, "totals", [SMEM, VMEM], [((8, SLICE, W + N), BF16)], 1 << 20, group, near
    )
    far = lax.all_to_all(totals, "seq", 0, 0, axis_index_groups=FAR, tiled=True)
    (enters,) = call(
        enter_kernel, "enters", [SMEM, VMEM, VMEM], [((GROUP, SLICE, 2 * W), BF16)], 1 << 20, group, near, far
    )
    enter = lax.all_to_all(enters, "seq", 0, 0, axis_index_groups=NEAR, tiled=True).reshape(N, 2 * W)
    hidden, part = call(
        mix_kernel,
        "mix",
        [SMEM, VMEM, VMEM, VMEM, VMEM, VMEM, VMEM],
        [((L, W), BF16), ((XS, L, W), BF16)],
        1 << 29,
        core, inner, gates, query, enter, cols, out_weight,
    )
    got = lax.ppermute(part, "tp", SWAP)
    (paired,) = call(
        pair_kernel, "pair", [SMEM, VMEM, VMEM, VMEM], [((XS, L, W), BF16)], 1 << 28, core, hidden, out_weight, got
    )
    pieces = lax.all_to_all(paired, "tp", 0, 0, axis_index_groups=X_GROUPS, tiled=True)
    return jnp.sum(pieces.astype(F32), axis=0).astype(BF16)


def solution(mesh):
    in_specs = (
        P("seq", "tp"),
        P(None, None, "tp"),
        P(None, "tp"),
        P(None, None, "tp"),
        P(None, "tp"),
        P("tp"),
        P("tp"),
        P("tp", None),
    )
    out_specs = P("seq", "tp")
    return jax.shard_map(shards, mesh=mesh, in_specs=in_specs, out_specs=out_specs, check_vma=False)
```

time: 525 us -> 118 us (0.22)
  waiting for transfers between devices: 218 us -> 9.99 us
  other arithmetic: 128 us -> 1.88 us
  blocking collectives: 128 us -> 64.2 us
  starting transfers between devices: 0.16 us -> 22.7 us
  matrix products: 19.7 us -> 0 us
  between operations: 13.3 us -> 0.16 us
  Pallas kernels: 0 us -> 11.5 us
    all_gather x4 -> x0, waiting for transfers between devices: 174 us -> none  [the longest x2 101 us: carried_in(): pieces = jax.tree.map(lambda part: lax.all_gather(part, axis), value)]
    all_gather x2 -> x0, blocking collectives: 128 us -> none  [carried_in(): pieces = jax.tree.map(lambda part: lax.all_gather(part, axis), value)]
    select_n x126 -> x0, other arithmetic: 126 us -> none  [lap(): jnp.where(position < mine, new, old)]
    all_to_all x0 -> x3, blocking collectives: none -> 64.2 us  [the longest x1 26.2 us: shards(): far = lax.all_to_all(totals, 'seq', 0, 0, axis_index_groups=FAR, tiled=True)]
    reduce_scatter x1 -> x0, waiting for transfers between devices: 42.1 us -> none  [shards(): lax.psum_scatter(partial_terms.astype(jnp.bfloat16), 'tp', scatter_dimens...]
    dot_general x12 -> x0, matrix products: 19.7 us -> none  [the longest x1 2.9 us: shards(): jnp.einsum('hts,shp->thp', forward_weights, values, preferred_element_typ...]
    ppermute x0 -> x2, starting transfers between devices: none -> 13.8 us  [the longest x1 7.5 us: shards(): theirs = lax.ppermute(mine, 'tp', SWAP)]
    pallas_call x0 -> x6, Pallas kernels: none -> 11.5 us  [call(): pl.pallas_call(kernel, name=name, in_specs=ins, out_specs=[VMEM] * len(ou...]
  transfers between devices with their start and end apart: 5 -> 4, of which waited for: 5 -> 3; matrix products, arithmetic and copies ran while one was open for 15% -> 3% of each run, Pallas kernels for 0% -> 3%
where the time goes in v1:
time: 118 us; the launch traced here: 117 us
  blocking collectives  64.2 us (54%)
  starting transfers between devices  22.7 us (19%)
  Pallas kernels  11.5 us (10%)
  waiting for transfers between devices  9.99 us (8%)
  local copies, waits for them, and re-layouts  7.04 us (6%)
  other arithmetic  1.88 us (2%)
    all_to_all x1, blocking collectives, shards(): far = lax.all_to_all(totals, 'seq', 0, 0, axis_index_groups=FAR, tiled=True)  26.2 us
    all_to_all x1, blocking collectives, shards(): lax.all_to_all(payload, 'tp', 0, 0, axis_index_groups=X_GROUPS, tiled=True)  20.7 us
    all_to_all x1, blocking collectives, shards(): lax.all_to_all(paired, 'tp', 0, 0, axis_index_groups=X_GROUPS, tiled=True)  17.3 us
    pallas_call x6, Pallas kernels, call(): pl.pallas_call(kernel, name=name, in_specs=ins, out_specs=[VMEM] * len(ou...  11.5 us
    ppermute x1, starting transfers between devices, shards(): theirs = lax.ppermute(mine, 'tp', SWAP)  7.5 us
    unnamed x16, local copies, waits for them, and re-layouts  6.9 us
    ppermute x1, starting transfers between devices, shards(): got = lax.ppermute(part, 'tp', SWAP)  6.31 us
    all_to_all x1, waiting for transfers between devices, shards(): lax.all_to_all(message, 'seq', 0, 0, axis_index_groups=NEAR, tiled=True)  5.61 us
  transfers between devices with their start and end apart: 4, of which 3 were waited for; matrix products, arithmetic and copies ran while one was open for 3% of the time, Pallas kernels for 3%

profile of v1, /device:TPU:1, one launch (start us, length us, event | category | flops | bytes accessed | tf_op | source)
XLA Modules:
  0.0 117.5 jit_solution(734176622758215964)
XLA Ops:
  0.0 0.9 copy.10
  1.0 1.0 pad_maximum_fusion
  1.9 0.1 broadcast_in_dim.13
  2.1 0.0 copy-start.6
  2.1 20.7 %all_to_all.25.a_ref = bf16[4,768,256]{2,1,0:T(8,128)(2,1)S(1)} all-to-all(bf16[4,768,256]{2,1,0:T(8,128)(2,1)S(1)} %broadcast_in_dim.13), channel_id=1, replica_groups={{0,2,4,6},{1,3,5,7},{8,10,12,14},{9,11,13,15},{16,18,20,22},{17,19,21,2..., dimensions={0} | all-to-all | bytes 3145728 | tf_op jit(solution)/shard_map/all_to_all | solution.py:255
  22.8 7.5 %collective-permute-start = (bf16[4,768,256]{2,1,0:T(8,128)(2,1)S(1)}, bf16[4,768,256]{2,1,0:T(8,128)(2,1)S(1)}, u32[]{:S(2)}, u32[]{:S(2)}) collective-permute-start(bf16[4,768,256]{2,1,0:T(8,128)(2,1)S(1)} %all_to_all.25.a_ref), channel_id=1, source_target_pairs={{0,1},{1,0},{2,3},{3,2},{4,5},{5,4},{6,7},{7,6},{8,9},{9,8},{10,11... | collective-permute-start | bytes 4718600 | tf_op jit(solution)/shard_map/ppermute | solution.py:256
  30.3 0.0 copy-done.6
  30.3 0.0 copy-start.3
  30.3 0.0 copy-start.4
  30.3 3.4 %copy.11 = bf16[256,8,2,256]{3,1,2,0:T(8,128)(2,1)} copy(bf16[256,8,2,256]{3,2,1,0:T(2,128)(2,1)} %bitcast.13) | data formatting | bytes 4194304
  33.7 0.0 collective-permute-done.b_ref
  33.7 0.0 copy-start.1
  33.7 1.1 copy-done.1
  34.9 0.0 copy-done.3
  34.9 0.0 copy-done.4
  34.9 0.0 copy-start.2
  34.9 1.4 %copy-done.2 = bf16[4,768,256]{2,1,0:T(8,128)(2,1)S(1)} copy-done((bf16[4,768,256]{2,1,0:T(8,128)(2,1)S(1)}, bf16[4,768,256]{2,1,0:T(8,128)(2,1)}, u32[]{:S(2)}) %copy-start.2) | copy-done | bytes 1572888
  36.3 0.0 copy-start.5
  36.3 5.4 %project.1 = (bf16[512,256]{1,0:T(8,128)(2,1)S(1)}, f32[512,256]{1,0:T(8,128)S(1)}, bf16[512,128]{1,0:T(8,128)(2,1)S(1)}, bf16[128,512]{1,0:T(8,128)(2,1)S(1)}, ...) custom-call(s32[1]{0:T(128)} %bitcast.core_ref, f32[2,4]{1,0:T(2,128)S(1)} %copy-done.3, ...), custom_call_target="tpu_custom_call" | custom-call | flops 2147483648 | bytes 2097152 | tf_op jit(solution)/shard_map/project/pallas_call | solution.py:238
  41.7 5.5 %all-to-all-start.1 = ((bf16[8,16,640]{2,1,0:T(8,128)(2,1)}), bf16[8,16,640]{2,1,0:T(8,128)(2,1)S(1)}, u32[]{:S(2)}, u32[]{:S(2)}) async-start(bf16[8,16,640]{2,1,0:T(8,128)(2,1)} %get-tuple-element.20), calls=%async_computation.1 | async-start | bytes 327680 | tf_op jit(solution)/shard_map/all_to_all | solution.py:275
  47.2 5.6 %all-to-all-done.1.got_ref = bf16[8,16,640]{2,1,0:T(8,128)(2,1)S(1)} async-done(((bf16[8,16,640]{2,1,0:T(8,128)(2,1)}), bf16[8,16,640]{2,1,0:T(8,128)(2,1)S(1)}, u32[]{:S(2)}, u32[]{:S(2)}) %all-to-all-start.1) | async-done | bytes 163872 | tf_op jit(solution)/shard_map/all_to_all | solution.py:275
  52.9 0.2 totals.1
  53.1 26.2 %all_to_all.26.far_ref = bf16[8,16,384]{2,1,0:T(8,128)(2,1)S(1)} all-to-all(bf16[8,16,384]{2,1,0:T(8,128)(2,1)S(1)} %totals.1), channel_id=1, replica_groups={{0,64,128,192,256,320,384,448},{8,72,136,200,264,328,392,456},{16,80,14..., dimensions={0} | all-to-all | bytes 196608 | tf_op jit(solution)/shard_map/all_to_all | solution.py:287
  79.3 0.9 enters.1
  80.2 3.4 %all-to-all-start.3 = ((bf16[8,16,512]{2,1,0:T(8,128)(2,1)}), bf16[8,16,512]{2,1,0:T(8,128)(2,1)S(1)}, u32[]{:S(2)}, u32[]{:S(2)}) async-start(bf16[8,16,512]{2,1,0:T(8,128)(2,1)} %enters.1), calls=%async_computation.3 | async-start | bytes 262144 | tf_op jit(solution)/shard_map/all_to_all | solution.py:291
  83.6 0.0 copy-done.5
  83.6 0.0 copy-start
  83.6 3.2 %inside.1.inner_ref = f32[512,256]{1,0:T(8,128)S(1)} custom-call(f32[4]{0:T(128)S(1)} %copy-done.5, bf16[512,128]{1,0:T(8,128)(2,1)S(1)} %get-tuple-element.14.query_ref, bf16[128,512]{1,0:T(8,128)(2,1)S(1)} %get-tuple-element.15.key_ref, bf16[512,256]{1,0:T(8,128)(2,1)S(1)} %get-tuple-element.16.values_ref, f32[48,512]{1,0:T(8,128)S(1)} %get-tuple-element.17.rows_ref, ...), custom_call_target="tpu_custom_call" | custom-call | flops 2147483648 | bytes 2097152 | tf_op jit(solution)/shard_map/inside/pallas_call | solution.py:238
  86.8 2.1 %all-to-all-done.3 = bf16[8,16,512]{2,1,0:T(8,128)(2,1)S(1)} async-done(((bf16[8,16,512]{2,1,0:T(8,128)(2,1)}), bf16[8,16,512]{2,1,0:T(8,128)(2,1)S(1)}, u32[]{:S(2)}, u32[]{:S(2)}) %all-to-all-start.3) | async-done | bytes 131104 | tf_op jit(solution)/shard_map/all_to_all | solution.py:291
  88.9 0.0 copy-done
  88.9 1.3 %mix.1 = (bf16[512,256]{1,0:T(8,128)(2,1)S(1)}, bf16[4,512,256]{2,1,0:T(8,128)(2,1)S(1)}) custom-call(s32[1]{0:T(128)} %bitcast.core_ref, f32[512,256]{1,0:T(8,128)S(1)} %inside.1.inner_ref, f32[512,256]{1,0:T(8,128)S(1)} %get-tuple-element.19.gates_ref, bf16[512,128]{1,0:T(8,128)(2,1)S(1)} %get-tuple-element.14.query_ref, bf16[128,512]{1,0:T(8,128)(2,1)S(1)} %bitcast.12, ...), custom_call_target="tpu_custom_call" | custom-call | flops 536870912 | bytes 2097152 | tf_op jit(solution)/shard_map/mix/pallas_call | solution.py:238
  90.2 6.3 %collective-permute-start.1 = (bf16[4,512,256]{2,1,0:T(8,128)(2,1)S(1)}, bf16[4,512,256]{2,1,0:T(8,128)(2,1)S(1)}, u32[]{:S(2)}, u32[]{:S(2)}) collective-permute-start(bf16[4,512,256]{2,1,0:T(8,128)(2,1)S(1)} %get-tuple-element.22), channel_id=1, source_target_pairs={{0,1},{1,0},{2,3},{3,2},{4,5},{5,4},{6,7},{7,6},{8,9},{9,8},{10,11... | collective-permute-start | bytes 3145736 | tf_op jit(solution)/shard_map/ppermute | solution.py:300
  96.6 2.3 %collective-permute-done.1.got_ref = bf16[4,512,256]{2,1,0:T(8,128)(2,1)S(1)} collective-permute-done((bf16[4,512,256]{2,1,0:T(8,128)(2,1)S(1)}, bf16[4,512,256]{2,1,0:T(8,128)(2,1)S(1)}, u32[]{:S(2)}, u32[]{:S(2)}) %collective-permute-start.1) | collective-permute-done | bytes 1048608 | tf_op jit(solution)/shard_map/ppermute | solution.py:300
  98.8 0.5 pair.1
  99.3 17.3 %all_to_all.27 = bf16[4,512,256]{2,1,0:T(8,128)(2,1)S(1)} all-to-all(bf16[4,512,256]{2,1,0:T(8,128)(2,1)S(1)} %pair.1), channel_id=1, replica_groups={{0,2,4,6},{1,3,5,7},{8,10,12,14},{9,11,13,15},{16,18,20,22},{17,19,21,2..., dimensions={0} | all-to-all | bytes 2097152 | tf_op jit(solution)/shard_map/all_to_all | solution.py:304
  116.6 0.9 reduce_sum.12
  (3 shorter events, 0.0 us)
Async XLA Ops:
  2.1 28.2 %copy-start.6 = (bf16[2,2048,4]{1,2,0:T(4,128)(2,1)S(1)}, bf16[2,2048,4]{1,2,0:T(4,128)(2,1)}, u32[]{:S(2)}) copy-start(bf16[2,2048,4]{1,2,0:T(4,128)(2,1)} %param.11) | copy-start | bytes 98308
  22.8 11.0 %collective-permute-start = (bf16[4,768,256]{2,1,0:T(8,128)(2,1)S(1)}, bf16[4,768,256]{2,1,0:T(8,128)(2,1)S(1)}, u32[]{:S(2)}, u32[]{:S(2)}) collective-permute-start(bf16[4,768,256]{2,1,0:T(8,128)(2,1)S(1)} %all_to_all.25.a_ref), channel_id=1, source_target_pairs={{0,1},{1,0},{2,3},{3,2},{4,5},{5,4},{6,7},{7,6},{8,9},{9,8},{10,11... | collective-permute-start | bytes 4718600 | tf_op jit(solution)/shard_map/ppermute | solution.py:256
  30.3 4.6 %copy-start.3 = (f32[2,4]{1,0:T(2,128)S(1)}, f32[2,4]{1,0:T(2,128)}, u32[]{:S(2)}) copy-start(f32[2,4]{1,0:T(2,128)} %bias_ref.1) | copy-start | bytes 100
  30.3 4.6 %copy-start.4 = (f32[4]{0:T(128)S(1)}, f32[4]{0:T(128)}, u32[]{:S(2)}) copy-start(f32[4]{0:T(128)} %rate_ref.1) | copy-start | bytes 52
  33.7 1.2 copy-start.1
  34.9 1.4 %copy-start.2 = (bf16[4,768,256]{2,1,0:T(8,128)(2,1)S(1)}, bf16[4,768,256]{2,1,0:T(8,128)(2,1)}, u32[]{:S(2)}) copy-start(bf16[4,768,256]{2,1,0:T(8,128)(2,1)} %copy-done.1) | copy-start | bytes 4718596
  36.3 47.3 %copy-start.5 = (f32[4]{0:T(128)S(1)}, f32[4]{0:T(128)}, u32[]{:S(2)}) copy-start(f32[4]{0:T(128)} %skip_ref.1) | copy-start | bytes 52
  41.7 11.2 %all-to-all-start.1 = ((bf16[8,16,640]{2,1,0:T(8,128)(2,1)}), bf16[8,16,640]{2,1,0:T(8,128)(2,1)S(1)}, u32[]{:S(2)}, u32[]{:S(2)}) async-start(bf16[8,16,640]{2,1,0:T(8,128)(2,1)} %get-tuple-element.20), calls=%async_computation.1 | async-start | bytes 327680 | tf_op jit(solution)/shard_map/all_to_all | solution.py:275
  80.2 8.7 %all-to-all-start.3 = ((bf16[8,16,512]{2,1,0:T(8,128)(2,1)}), bf16[8,16,512]{2,1,0:T(8,128)(2,1)S(1)}, u32[]{:S(2)}, u32[]{:S(2)}) async-start(bf16[8,16,512]{2,1,0:T(8,128)(2,1)} %enters.1), calls=%async_computation.3 | async-start | bytes 262144 | tf_op jit(solution)/shard_map/all_to_all | solution.py:291
  83.6 5.4 %copy-start = (bf16[256,2048]{1,0:T(8,128)(2,1)S(1)}, bf16[256,2048]{1,0:T(8,128)(2,1)}, u32[]{:S(2)}) copy-start(bf16[256,2048]{1,0:T(8,128)(2,1)} %w_ref.3) | copy-start | bytes 3145732
  90.2 8.6 %collective-permute-start.1 = (bf16[4,512,256]{2,1,0:T(8,128)(2,1)S(1)}, bf16[4,512,256]{2,1,0:T(8,128)(2,1)S(1)}, u32[]{:S(2)}, u32[]{:S(2)}) collective-permute-start(bf16[4,512,256]{2,1,0:T(8,128)(2,1)S(1)} %get-tuple-element.22), channel_id=1, source_target_pairs={{0,1},{1,0},{2,3},{3,2},{4,5},{5,4},{6,7},{7,6},{8,9},{9,8},{10,11... | collective-permute-start | bytes 3145736 | tf_op jit(solution)/shard_map/ppermute | solution.py:300

commit v2 on v1

v2 whole, which is shorter than its diff:
```python
import jax
import jax.numpy as jnp
from jax import lax
from jax.experimental import pallas as pl
from jax.experimental.pallas import tpu as pltpu
from jax.sharding import PartitionSpec as P

F32 = jnp.float32
BF16 = jnp.bfloat16
L = 512
D = 2048
W = 256
H = 4
HD = 64
N = 128
XS = 4
GROUP = 8
SLICE = N // GROUP

X_GROUPS = [[2 * x + c for x in range(XS)] for c in range(2)]
PAIRS = [[2 * x, 2 * x + 1] for x in range(XS)]
SWAP = [(i, i ^ 1) for i in range(8)]
NEAR = [[GROUP * g + j for j in range(GROUP)] for g in range(8)]
FAR = [[GROUP * g + j for g in range(8)] for j in range(GROUP)]

VMEM = pl.BlockSpec(memory_space=pltpu.VMEM)
SMEM = pl.BlockSpec(memory_space=pltpu.SMEM)
HBM = pl.BlockSpec(memory_space=pltpu.HBM)
NN = (((1,), (0,)), ((), ()))
NT = (((1,), (1,)), ((), ()))


def dot(a, b, dims=NN):
    return lax.dot_general(a, b, dims, preferred_element_type=F32)


def iota(shape, axis):
    return lax.broadcasted_iota(jnp.int32, shape, axis)


def spread(width, base, copies):
    row = iota((N, width), 0)
    want = iota((N, width), 1) // HD + base
    hit = row == want
    for q in range(1, copies):
        hit = hit | (row == want + 8 * q)
    return hit.astype(BF16)


def widen(cols, base, width):
    pick = spread(width, base, 1)
    high = cols.astype(BF16)
    low = (cols - high.astype(F32)).astype(BF16)
    return dot(high, pick) + dot(low, pick)


def column(ref, rows):
    index = iota((2 * H, 1), 0)
    out = jnp.zeros((2 * H, 1), F32)
    for i in range(2 * H):
        out = jnp.where(index == i, rows(ref, i), out)
    return out


def prep_kernel(tokens_ref, bc_ref, out_ref, sems):
    copies = []
    for x in range(XS):
        copies.append(pltpu.make_async_copy(tokens_ref, out_ref.at[x, pl.ds(0, L)], sems.at[len(copies)]))
        for b in range(8):
            copies.append(
                pltpu.make_async_copy(
                    bc_ref.at[:, pl.ds(W * b, W)], out_ref.at[x, pl.ds(L + 32 * b, 32)], sems.at[len(copies)]
                )
            )
    for copy in copies:
        copy.start()
    for copy in copies:
        copy.wait()


def columns_kernel(core_ref, w_ref, out_ref):
    for x in range(XS):
        at = pl.multiple_of((2 * x + 1 - core_ref[0]) * W, W)
        out_ref[:, W * x : W * (x + 1)] = w_ref[:, pl.ds(at, W)]


def bc_columns(ref, first, j):
    row = pl.multiple_of(L + j * 32, 32)
    return [ref[x, pl.ds(row, 32), :] for x in (first, first + 1)]


def wide_part(ref, w_ref, c):
    total = None
    for x in range(XS):
        rows = pl.ds(pl.multiple_of((2 * x + c) * W, W), W)
        term = dot(ref[x, 0:L, :], w_ref[rows, :])
        total = term if total is None else total + term
    return total


def narrow_part(ref, refs, d_ref, c):
    total = None
    for x in range(XS):
        j = 2 * x + c
        pieces = [piece for r in refs for piece in bc_columns(r, 0, j)]
        if d_ref is not None:
            pieces.append(d_ref[:, pl.ds(pl.multiple_of(j * W, W), W)])
        term = dot(jnp.concatenate(pieces, axis=0), ref[x, 0:L, :], NT)
        total = term if total is None else total + term
    return total


def query_part(ref, refs, c):
    total = None
    for x in range(XS):
        pieces = [piece for r in refs for piece in bc_columns(r, 2, 2 * x + c)]
        term = dot(ref[x, 0:L, :], jnp.concatenate(pieces, axis=0), NT)
        total = term if total is None else total + term
    return total


def half_kernel(core_ref, a_ref, w_ref, d_ref, wide_ref, narrow_ref, steps_ref, high_ref):
    c = core_ref[0]
    high_ref[...] = jnp.zeros((SLICE, D), F32)
    for i in range(2):
        high_ref[H * i : H * (i + 1), :] = d_ref[i].astype(F32)
    steps_ref[...] = high_ref[...].astype(BF16)
    wide_ref[...] = wide_part(a_ref, w_ref, c)
    narrow_ref[...] = narrow_part(a_ref, (a_ref,), steps_ref, c)


def project_kernel(
    core_ref, bias_ref, rate_ref, a_ref, b_ref, w_ref, d_ref, half_ref, narrow_ref,
    values_ref, gates_ref, query_ref, key_ref, rows_ref, message_ref,
):
    c = core_ref[0]
    later = narrow_part(b_ref, (a_ref, b_ref), d_ref, 1 - c)
    earlier = narrow_ref[...]
    key = jnp.concatenate(
        [earlier[0:64] + later[0:64], narrow_part(a_ref, (b_ref,), None, c) + later[64:128]], axis=0
    ).astype(BF16)
    key_ref[...] = key
    both = half_ref[...] + wide_part(b_ref, w_ref, 1 - c)
    values = both[:, :W].astype(BF16)
    values_ref[...] = values
    gates_ref[...] = both[:, W:]
    query_ref[...] = (query_part(a_ref, (a_ref, b_ref), c) + query_part(b_ref, (a_ref, b_ref), 1 - c)).astype(BF16)
    raw = (earlier[64:72] + later[128:136]) + column(bias_ref, lambda r, i: r[i // H, i % H])
    steps = jnp.maximum(raw, 0.0) + jnp.log1p(jnp.exp(-jnp.abs(raw)))
    logs = -column(rate_ref, lambda r, i: r[i % H]) * steps
    p1 = logs.astype(BF16)
    rest = logs - p1.astype(F32)
    p2 = rest.astype(BF16)
    p3 = (rest - p2.astype(F32)).astype(BF16)
    running = (iota((L, L), 0) <= iota((L, L), 1)).astype(BF16)
    parts = jnp.concatenate([p1.astype(F32), p2.astype(F32), p3.astype(F32), jnp.zeros((8, L), F32)], axis=0)
    summed = dot(parts.astype(BF16), running)
    upto = summed[0:8] + summed[8:16] + summed[16:24]
    before = upto - logs
    total = upto[:, L - 1 : L]
    forward = iota((2 * H, L), 0) < H
    scale = jnp.exp(jnp.where(forward, total - upto, before)) * steps
    reach = jnp.exp(jnp.where(forward, before, total - upto))
    rows_ref[...] = jnp.concatenate([upto, before, steps, reach], axis=0)

    wide = key.astype(F32)
    scaled = jnp.concatenate([(wide * scale[i : i + 1]).astype(BF16) for i in range(2 * H)], axis=0)
    state = dot(scaled, values)
    head = iota((N, W), 1) // HD
    sides = []
    for first in (0, H):
        out = state[N * first : N * (first + 1)]
        for h in range(1, H):
            out = jnp.where(head == h, state[N * (first + h) : N * (first + h + 1)], out)
        sides.append(out.astype(BF16))
    lane = iota((2 * H, N), 1)
    mine_only = (iota((2 * H, N), 0) == lane % 8) & (lane < 16)
    last = jnp.sum(jnp.where(mine_only, total, 0.0), axis=0, keepdims=True)
    high = last.astype(BF16).astype(F32)
    extra = jnp.where(iota((1, N), 1) < 8, high, last - high)
    extra = jnp.broadcast_to(extra, (SLICE, N)).astype(BF16)
    for k in range(GROUP):
        for i in range(2):
            message_ref[k, :, W * i : W * (i + 1)] = sides[i][SLICE * k : SLICE * (k + 1)]
        message_ref[k, :, 2 * W : 2 * W + N] = extra


def inner_kernel(skip_ref, query_ref, key_ref, values_ref, rows_ref, inner_ref, cols_ref):
    cols_ref[...] = jnp.concatenate([rows_ref[...], jnp.zeros((N - 32, L), F32)], axis=0).T
    key = key_ref[...]
    values = values_ref[...]
    tile = 128
    lane = iota((tile, W), 1) // HD

    def body(i, carry):
        at = pl.ds(pl.multiple_of(i * tile, tile), tile)
        scores = dot(query_ref[at, :], key)
        t = iota((tile, L), 0) + i * tile
        s = iota((tile, L), 1)
        lower = s < t
        upper = s > t
        own = values_ref[at, :].astype(F32)
        gain = jnp.zeros((tile, W), F32)
        out = jnp.zeros((tile, W), F32)
        for h in range(H):
            gap = jnp.where(
                lower,
                cols_ref[at, 8 + h : 9 + h] - rows_ref[h : h + 1, :],
                rows_ref[12 + h : 13 + h, :] - cols_ref[at, H + h : H + h + 1],
            )
            step = jnp.where(lower, rows_ref[16 + h : 17 + h, :], rows_ref[20 + h : 21 + h, :])
            weight = jnp.where(lower | upper, scores * jnp.exp(gap) * step, 0.0).astype(BF16)
            out = jnp.where(lane == h, dot(weight, values), out)
            gain = jnp.where(lane == h, skip_ref[h], gain)
        inner_ref[at, :] = out + gain * own
        return carry

    lax.fori_loop(0, L // tile, body, 0)


def near_states(got_ref):
    extra = got_ref[:, :, 2 * W : 2 * W + N].reshape(GROUP * SLICE, N)
    decay = jnp.exp(dot(extra, spread(2 * W, 0, 2)))
    states = [got_ref[j, :, 0 : 2 * W].astype(F32) for j in range(GROUP)]
    decays = [decay[SLICE * j : SLICE * (j + 1)] for j in range(GROUP)]
    return states, decays


def totals_kernel(group_ref, got_ref, out_ref):
    g = group_ref[0]
    states, decays = near_states(got_ref)
    forward = states[0][:, :W]
    for j in range(1, GROUP):
        forward = decays[j][:, :W] * forward + states[j][:, :W]
    backward = states[GROUP - 1][:, W:]
    for j in range(GROUP - 2, -1, -1):
        backward = decays[j][:, W:] * backward + states[j][:, W:]
    log = jnp.zeros((SLICE, N), F32)
    for j in range(GROUP):
        log = log + got_ref[j, :, 2 * W : 2 * W + N].astype(F32)
    high = log.astype(BF16).astype(F32)
    log = (high + pltpu.roll(log - high, 16, 1)).astype(BF16)
    forward = forward.astype(BF16)
    backward = backward.astype(BF16)
    for q in range(8):
        out_ref[q, :, 0:W] = jnp.where(q > g, forward, backward)
        out_ref[q, :, W : W + N] = log


def enter_kernel(group_ref, got_ref, far_ref, out_ref):
    g = group_ref[0]
    states, decays = near_states(got_ref)
    extra = far_ref[:, :, W : W + N].reshape(8 * SLICE, N)
    decay = jnp.exp(dot(extra, spread(2 * W, 0, 4)))
    forward = jnp.zeros((SLICE, W), F32)
    backward = jnp.zeros((SLICE, W), F32)
    for q in range(8):
        rows = slice(SLICE * q, SLICE * (q + 1))
        forward = jnp.where(q < g, decay[rows, :W] * forward + far_ref[q, :, 0:W].astype(F32), forward)
    for q in range(7, -1, -1):
        rows = slice(SLICE * q, SLICE * (q + 1))
        backward = jnp.where(q > g, decay[rows, W:] * backward + far_ref[q, :, 0:W].astype(F32), backward)
    for j in range(GROUP):
        out_ref[j, :, 0:W] = forward.astype(BF16)
        forward = decays[j][:, :W] * forward + states[j][:, :W]
    for j in range(GROUP - 1, -1, -1):
        out_ref[j, :, W : 2 * W] = backward.astype(BF16)
        backward = decays[j][:, W:] * backward + states[j][:, W:]


def mix_kernel(inner_ref, gates_ref, query_ref, enter_ref, cols_ref, hidden_ref):
    carried = dot(query_ref[...], enter_ref[...]) * widen(cols_ref[...], 24, 2 * W)
    mix = inner_ref[...] + carried[:, :W] + carried[:, W:]
    gates = gates_ref[...]
    gated = mix * (gates / (1.0 + jnp.exp(-gates)))
    square = gated * gated
    same = (iota((W, W), 0) // HD == iota((W, W), 1) // HD).astype(BF16)
    high = square.astype(BF16)
    low = (square - high.astype(F32)).astype(BF16)
    power = (dot(high, same) + dot(low, same)) * (1.0 / HD)
    hidden_ref[...] = (gated * lax.rsqrt(power + 1e-05)).astype(BF16)


def pair_kernel(core_ref, hidden_ref, w_ref, other_ref, out_ref):
    c = core_ref[0]
    hidden = jnp.concatenate([hidden_ref[c], hidden_ref[1 - c]], axis=1)
    for x in range(XS):
        at = pl.ds(pl.multiple_of((2 * x + c) * W, W), W)
        out_ref[x] = dot(hidden, jnp.concatenate([w_ref[:, at], other_ref[:, W * x : W * (x + 1)]], axis=0)).astype(BF16)


def sum_kernel(pieces_ref, out_ref):
    total = pieces_ref[0].astype(F32) + pieces_ref[1].astype(F32)
    total = total + pieces_ref[2].astype(F32) + pieces_ref[3].astype(F32)
    out_ref[...] = total.astype(BF16)


def call(kernel, name, ins, outs, flops, *operands, touched=1 << 21, scratch=(), out_spec=VMEM):
    return pl.pallas_call(
        kernel,
        name=name,
        in_specs=ins,
        out_specs=[out_spec] * len(outs),
        scratch_shapes=scratch,
        out_shape=[jax.ShapeDtypeStruct(shape, kind) for shape, kind in outs],
        compiler_params=pltpu.CompilerParams(vmem_limit_bytes=20 << 20),
        cost_estimate=pl.CostEstimate(flops=flops, bytes_accessed=touched, transcendentals=1 << 16),
    )(*operands)


def shards(tokens, in_weight, bc_weight, dt_weight, dt_bias, decay_rate, skip_gain, out_weight):
    core = (lax.axis_index("tp").astype(jnp.int32) & 1)[None]
    group = (lax.axis_index("seq").astype(jnp.int32) >> 3)[None]
    (payload,) = call(
        prep_kernel,
        "payload",
        [HBM, HBM],
        [((XS, L + W, W), BF16)],
        1,
        tokens,
        bc_weight.T,
        touched=0,
        scratch=[pltpu.SemaphoreType.DMA((9 * XS,))],
        out_spec=HBM,
    )
    flat_weight = in_weight.reshape(D, 2 * W)
    steps_weight = dt_weight.transpose(0, 2, 1)
    mine = lax.all_to_all(payload, "tp", 0, 0, axis_index_groups=X_GROUPS, tiled=True)
    (other_weight,) = call(
        columns_kernel, "columns", [SMEM, VMEM], [((W, XS * W), BF16)], 1, core, out_weight
    )
    other_weight = lax.ppermute(other_weight, "tp", SWAP)
    mine, core, group, other_weight = lax.optimization_barrier((mine, core, group, other_weight))
    theirs = lax.ppermute(mine, "tp", SWAP)
    half, narrow, steps_weight = call(
        half_kernel,
        "half",
        [SMEM, VMEM, VMEM, VMEM],
        [((L, 2 * W), F32), ((80, L), F32), ((SLICE, D), BF16)],
        1 << 30,
        core, mine, flat_weight, steps_weight,
        scratch=[pltpu.VMEM((SLICE, D), F32)],
    )
    values, gates, query, key, rows, message = call(
        project_kernel,
        "project",
        [SMEM, SMEM, SMEM, VMEM, VMEM, VMEM, VMEM, VMEM, VMEM],
        [
            ((L, W), BF16),
            ((L, W), F32),
            ((L, N), BF16),
            ((N, L), BF16),
            ((32, L), F32),
            ((GROUP, SLICE, 2 * W + N), BF16),
        ],
        1 << 31,
        core, dt_bias, decay_rate, mine, theirs, flat_weight, steps_weight, half, narrow,
    )
    near = lax.all_to_all(message, "seq", 0, 0, axis_index_groups=NEAR, tiled=True)
    inner, cols = call(
        inner_kernel,
        "inside",
        [SMEM, VMEM, VMEM, VMEM, VMEM],
        [((L, W), F32), ((L, N), F32)],
        1 << 31,
        skip_gain, query, key, values, rows,
    )
    (totals,) = call(
        totals_kernel, "totals", [SMEM, VMEM], [((8, SLICE, W + N), BF16)], 1 << 20, group, near
    )
    far = lax.all_to_all(totals, "seq", 0, 0, axis_index_groups=FAR, tiled=True)
    far, inner, cols = lax.optimization_barrier((far, inner, cols))
    (enters,) = call(
        enter_kernel, "enters", [SMEM, VMEM, VMEM], [((GROUP, SLICE, 2 * W), BF16)], 1 << 20, group, near, far
    )
    enter = lax.all_to_all(enters, "seq", 0, 0, axis_index_groups=NEAR, tiled=True).reshape(N, 2 * W)
    (hidden,) = call(
        mix_kernel, "mix", [VMEM] * 5, [((L, W), BF16)], 1 << 28, inner, gates, query, enter, cols
    )
    hidden = lax.all_gather(hidden, "tp", axis_index_groups=PAIRS)
    (paired,) = call(
        pair_kernel, "pair", [SMEM, VMEM, VMEM, VMEM], [((XS, L, W), BF16)], 1 << 29, core, hidden, out_weight, other_weight
    )
    pieces = lax.all_to_all(paired, "tp", 0, 0, axis_index_groups=X_GROUPS, tiled=True)
    return call(sum_kernel, "sum", [VMEM], [((L, W), BF16)], 1 << 20, pieces)[0]


def solution(mesh):
    in_specs = (
        P("seq", "tp"),
        P(None, None, "tp"),
        P(None, "tp"),
        P(None, None, "tp"),
        P(None, "tp"),
        P("tp"),
        P("tp"),
        P("tp", None),
    )
    out_specs = P("seq", "tp")
    return jax.shard_map(shards, mesh=mesh, in_specs=in_specs, out_specs=out_specs, check_vma=False)
```

time: 118 us -> 112 us (0.949)
  blocking collectives: 64.2 us -> 42.5 us
  starting transfers between devices: 22.7 us -> 35.1 us
  waiting for transfers between devices: 9.99 us -> 14.7 us
  Pallas kernels: 11.5 us -> 13.5 us
  other arithmetic: 1.88 us -> 0 us
  local copies, waits for them, and re-layouts: 7.04 us -> 5.68 us
    all_to_all x2, blocking collectives: 46.9 us -> 19 us  [the longest x1 11.1 us: shards(): lax.all_to_all(message, 'seq', 0, 0, axis_index_groups=NEAR, tiled=True)]
    all_to_all x2, starting transfers between devices: 8.92 us -> 18.9 us  [the longest x1 13.9 us: shards(): far = lax.all_to_all(totals, 'seq', 0, 0, axis_index_groups=FAR, tiled=True)]
    all_gather x0 -> x1, blocking collectives: none -> 6.29 us  [shards(): hidden = lax.all_gather(hidden, 'tp', axis_index_groups=PAIRS)]
    all_to_all x2, waiting for transfers between devices: 7.72 us -> 13 us  [the longest x1 7.43 us: shards(): far = lax.all_to_all(totals, 'seq', 0, 0, axis_index_groups=FAR, tiled=True)]
    pallas_call x6 -> x10, Pallas kernels: 11.5 us -> 13.5 us  [call(): pl.pallas_call(kernel, name=name, in_specs=ins, out_specs=[out_spec] * le...]
    ppermute x1, starting transfers between devices: 6.31 us -> 7.53 us  [shards(): other_weight = lax.ppermute(other_weight, 'tp', SWAP)]
    unnamed x16 -> x23, local copies, waits for them, and re-layouts: 6.9 us -> 5.68 us
    ppermute x1, starting transfers between devices: 7.5 us -> 8.69 us  [shards(): theirs = lax.ppermute(mine, 'tp', SWAP)]
  transfers between devices with their start and end apart: 4 -> 4, of which waited for: 3 -> 3; matrix products, arithmetic and copies ran while one was open for 3% -> 2% of each run, Pallas kernels for 3% -> 4%
where the time goes in v2:
time: 112 us
  blocking collectives  42.5 us (38%)
  starting transfers between devices  35.1 us (31%)
  waiting for transfers between devices  14.7 us (13%)
  Pallas kernels  13.5 us (12%)
  local copies, waits for them, and re-layouts  5.68 us (5%)
    all_to_all x1, blocking collectives, shards(): lax.all_to_all(paired, 'tp', 0, 0, axis_index_groups=X_GROUPS, tiled=True)  17.3 us
    all_to_all x1, starting transfers between devices, shards(): far = lax.all_to_all(totals, 'seq', 0, 0, axis_index_groups=FAR, tiled=True)  13.9 us
    pallas_call x10, Pallas kernels, call(): pl.pallas_call(kernel, name=name, in_specs=ins, out_specs=[out_spec] * le...  13.5 us
    all_to_all x1, blocking collectives, shards(): lax.all_to_all(message, 'seq', 0, 0, axis_index_groups=NEAR, tiled=True)  11.1 us
    ppermute x1, starting transfers between devices, shards(): theirs = lax.ppermute(mine, 'tp', SWAP)  8.69 us
    all_to_all x1, blocking collectives, shards(): lax.all_to_all(enters, 'seq', 0, 0, axis_index_groups=NEAR, tiled=True)  7.82 us
    ppermute x1, starting transfers between devices, shards(): other_weight = lax.ppermute(other_weight, 'tp', SWAP)  7.53 us
    all_to_all x1, waiting for transfers between devices, shards(): far = lax.all_to_all(totals, 'seq', 0, 0, axis_index_groups=FAR, tiled=True)  7.43 us
  transfers between devices with their start and end apart: 4, of which 3 were waited for; matrix products, arithmetic and copies ran while one was open for 2% of the time, Pallas kernels for 4%

profile of v2, /device:TPU:1, one launch (start us, length us, event | category | flops | bytes accessed | tf_op | source)
XLA Modules:
  0.0 111.7 jit_solution(17294756494666917070)
XLA Ops:
  0.0 0.0 copy-start.1
  0.0 0.9 copy-done.1
  1.0 0.0 copy-start.2
  1.0 0.9 copy-done.2
  1.9 1.5 %payload.1 = bf16[4,768,256]{2,1,0:T(8,128)(2,1)} custom-call(bf16[512,256]{1,0:T(8,128)(2,1)S(1)} %copy-done.1, bf16[32,2048]{1,0:T(8,128)(2,1)S(1)} %bitcast.12), custom_call_target="tpu_custom_call" | custom-call | flops 1 | tf_op jit(solution)/shard_map/payload/pallas_call | solution.py:299
  3.4 0.0 copy-start
  3.4 5.0 %all-to-all-start = ((bf16[4,768,256]{2,1,0:T(8,128)(2,1)}), bf16[4,768,256]{2,1,0:T(8,128)(2,1)S(1)}, u32[]{:S(2)}, u32[]{:S(2)}) async-start(bf16[4,768,256]{2,1,0:T(8,128)(2,1)} %payload.1), calls=%async_computation | async-start | bytes 3145728 | tf_op jit(solution)/shard_map/all_to_all | solution.py:328
  8.4 0.0 copy-done
  8.4 0.1 columns.1
  8.4 7.5 %collective-permute-start = (bf16[256,1024]{1,0:T(8,128)(2,1)S(1)}, bf16[256,1024]{1,0:T(8,128)(2,1)}, u32[]{:S(2)}, u32[]{:S(2)}) collective-permute-start(bf16[256,1024]{1,0:T(8,128)(2,1)S(1)} %columns.1), channel_id=1, source_target_pairs={{0,1},{1,0},{2,3},{3,2},{4,5},{5,4},{6,7},{7,6},{8,9},{9,8},{10,11... | collective-permute-start | bytes 1572872 | tf_op jit(solution)/shard_map/ppermute | solution.py:332
  16.0 1.6 %collective-permute-done.other_ref = bf16[256,1024]{1,0:T(8,128)(2,1)} collective-permute-done((bf16[256,1024]{1,0:T(8,128)(2,1)S(1)}, bf16[256,1024]{1,0:T(8,128)(2,1)}, u32[]{:S(2)}, u32[]{:S(2)}) %collective-permute-start) | collective-permute-done | bytes 524320 | tf_op jit(solution)/shard_map/ppermute | solution.py:332
  17.6 5.6 %all-to-all-done.a_ref = bf16[4,768,256]{2,1,0:T(8,128)(2,1)S(1)} async-done(((bf16[4,768,256]{2,1,0:T(8,128)(2,1)}), bf16[4,768,256]{2,1,0:T(8,128)(2,1)S(1)}, u32[]{:S(2)}, u32[]{:S(2)}) %all-to-all-start) | async-done | bytes 1572896 | tf_op jit(solution)/shard_map/all_to_all | solution.py:328
  23.2 8.7 %collective-permute-start.1 = (bf16[4,768,256]{2,1,0:T(8,128)(2,1)S(1)}, bf16[4,768,256]{2,1,0:T(8,128)(2,1)S(1)}, u32[]{:S(2)}, u32[]{:S(2)}) collective-permute-start(bf16[4,768,256]{2,1,0:T(8,128)(2,1)S(1)} %all-to-all-done.a_ref), channel_id=1, source_target_pairs={{0,1},{1,0},{2,3},{3,2},{4,5},{5,4},{6,7},{7,6},{8,9},{9,8},{10,11... | collective-permute-start | bytes 4718600 | tf_op jit(solution)/shard_map/ppermute | solution.py:334
  31.9 0.0 copy-start.3
  31.9 2.0 %copy.9 = bf16[256,8,2,256]{3,1,2,0:T(8,128)(2,1)S(1)} copy(bf16[256,8,2,256]{3,2,1,0:T(2,128)(2,1)} %bitcast.14) | data formatting | bytes 4194304
  34.0 0.0 copy-done.3
  34.0 0.0 copy-start.4
  34.0 0.0 copy-start.5
  34.0 1.0 half.1
  35.0 0.0 collective-permute-done.1.b_ref
  35.0 0.0 copy-done.4
  35.0 0.0 copy-done.5
  35.0 0.0 copy-start.6
  35.0 3.0 %project.1 = (bf16[512,256]{1,0:T(8,128)(2,1)S(1)}, f32[512,256]{1,0:T(8,128)S(1)}, bf16[512,128]{1,0:T(8,128)(2,1)S(1)}, bf16[128,512]{1,0:T(8,128)(2,1)S(1)}, ...) custom-call(s32[1]{0:T(128)} %bitcast.1.core_ref, f32[2,4]{1,0:T(2,128)S(1)} %copy-done.4, f32[4]{0:T(128)S(1)} %copy-done.5, ...), custom_call_target="tpu_custom_call" | custom-call | flops 2147483648 | bytes 2097152 | tf_op jit(solution)/shard_map/project/pallas_call | solution.py:299
  38.0 0.0 copy-start.7
  38.0 0.0 copy-start.9
  38.0 11.1 %all_to_all.25.got_ref = bf16[8,16,640]{2,1,0:T(8,128)(2,1)S(1)} all-to-all(bf16[8,16,640]{2,1,0:T(8,128)(2,1)S(1)} %get-tuple-element.29), channel_id=1, replica_groups={{0,8,16,24,32,40,48,56},{64,72,80,88,96,104,112,120},{128,136,144,152,1..., dimensions={0} | all-to-all | bytes 327680 | tf_op jit(solution)/shard_map/all_to_all | solution.py:359
  49.2 0.0 copy-done.7
  49.2 0.0 copy-done.9
  49.2 0.8 totals.1
  50.0 13.9 %all-to-all-start.2 = ((bf16[8,16,384]{2,1,0:T(8,128)(2,1)}), bf16[8,16,384]{2,1,0:T(8,128)(2,1)S(1)}, u32[]{:S(2)}, u32[]{:S(2)}) async-start(bf16[8,16,384]{2,1,0:T(8,128)(2,1)} %totals.1), calls=%async_computation.2 | async-start | bytes 196608 | tf_op jit(solution)/shard_map/all_to_all | solution.py:371
  63.9 0.0 copy-done.6
  63.9 0.0 copy-start.8
  63.9 0.9 copy-done.8
  64.8 0.0 copy-start.10
  64.8 0.8 copy-done.10
  65.7 3.3 %inside.1 = (f32[512,256]{1,0:T(8,128)S(1)}, f32[512,128]{1,0:T(8,128)S(1)}) custom-call(f32[4]{0:T(128)S(1)} %copy-done.6, bf16[512,128]{1,0:T(8,128)(2,1)S(1)} %get-tuple-element.30.query_ref, bf16[128,512]{1,0:T(8,128)(2,1)S(1)} %copy-done.8, bf16[512,256]{1,0:T(8,128)(2,1)S(1)} %get-tuple-element.32.values_ref, f32[32,512]{1,0:T(8,128)S(1)} %copy-done.10), custom_call_target="tpu_custom_call" | custom-call | flops 2147483648 | bytes 2097152 | tf_op jit(solution)/shard_map/inside/pallas_call | solution.py:299
  69.0 7.4 %all-to-all-done.2.far_ref = bf16[8,16,384]{2,1,0:T(8,128)(2,1)S(1)} async-done(((bf16[8,16,384]{2,1,0:T(8,128)(2,1)}), bf16[8,16,384]{2,1,0:T(8,128)(2,1)S(1)}, u32[]{:S(2)}, u32[]{:S(2)}) %all-to-all-start.2) | async-done | bytes 98336 | tf_op jit(solution)/shard_map/all_to_all | solution.py:371
  76.4 0.3 enters.1
  76.7 7.8 %all_to_all.26 = bf16[8,16,512]{2,1,0:T(8,128)(2,1)S(1)} all-to-all(bf16[8,16,512]{2,1,0:T(8,128)(2,1)S(1)} %enters.1), channel_id=1, replica_groups={{0,8,16,24,32,40,48,56},{64,72,80,88,96,104,112,120},{128,136,144,152,1..., dimensions={0} | all-to-all | bytes 262144 | tf_op jit(solution)/shard_map/all_to_all | solution.py:376
  84.5 1.0 mix.1
  85.5 6.3 %all-gather = bf16[1024,256]{1,0:T(8,128)(2,1)S(1)} all-gather(bf16[512,256]{1,0:T(8,128)(2,1)S(1)} %mix.1), channel_id=2, replica_groups={{0,1},{2,3},{4,5},{6,7},{8,9},{10,11},{12,13},{14,15},{16,17},{18,19},{..., dimensions={0}, use_global_device_ids=true | all-gather | bytes 786432 | tf_op jit(solution)/shard_map/all_gather | solution.py:380
  91.8 1.8 %pair.1 = bf16[4,512,256]{2,1,0:T(8,128)(2,1)S(1)} custom-call(s32[1]{0:T(128)} %bitcast.1.core_ref, bf16[2,512,256]{2,1,0:T(8,128)(2,1)S(1)} %bitcast.10, bf16[256,2048]{1,0:T(8,128)(2,1)S(1)} %copy-done, bf16[256,1024]{1,0:T(8,128)(2,1)} %collective-permute-done.other_ref), custom_call_target="tpu_custom_call" | custom-call | flops 536870912 | bytes 2097152 | tf_op jit(solution)/shard_map/pair/pallas_call | solution.py:299
  93.6 17.3 %all_to_all.27.pieces_ref = bf16[4,512,256]{2,1,0:T(8,128)(2,1)S(1)} all-to-all(bf16[4,512,256]{2,1,0:T(8,128)(2,1)S(1)} %pair.1), channel_id=1, replica_groups={{0,2,4,6},{1,3,5,7},{8,10,12,14},{9,11,13,15},{16,18,20,22},{17,19,21,2..., dimensions={0} | all-to-all | bytes 2097152 | tf_op jit(solution)/shard_map/all_to_all | solution.py:384
  110.8 0.8 sum.1
Async XLA Ops:
  0.0 0.9 copy-start.1
  1.0 0.9 copy-start.2
  3.4 5.0 %copy-start = (bf16[256,2048]{1,0:T(8,128)(2,1)S(1)}, bf16[256,2048]{1,0:T(8,128)(2,1)}, u32[]{:S(2)}) copy-start(bf16[256,2048]{1,0:T(8,128)(2,1)} %w_ref.3) | copy-start | bytes 3145732
  3.4 19.9 %all-to-all-start = ((bf16[4,768,256]{2,1,0:T(8,128)(2,1)}), bf16[4,768,256]{2,1,0:T(8,128)(2,1)S(1)}, u32[]{:S(2)}, u32[]{:S(2)}) async-start(bf16[4,768,256]{2,1,0:T(8,128)(2,1)} %payload.1), calls=%async_computation | async-start | bytes 3145728 | tf_op jit(solution)/shard_map/all_to_all | solution.py:328
  8.4 9.2 %collective-permute-start = (bf16[256,1024]{1,0:T(8,128)(2,1)S(1)}, bf16[256,1024]{1,0:T(8,128)(2,1)}, u32[]{:S(2)}, u32[]{:S(2)}) collective-permute-start(bf16[256,1024]{1,0:T(8,128)(2,1)S(1)} %columns.1), channel_id=1, source_target_pairs={{0,1},{1,0},{2,3},{3,2},{4,5},{5,4},{6,7},{7,6},{8,9},{9,8},{10,11... | collective-permute-start | bytes 1572872 | tf_op jit(solution)/shard_map/ppermute | solution.py:332
  23.2 11.8 %collective-permute-start.1 = (bf16[4,768,256]{2,1,0:T(8,128)(2,1)S(1)}, bf16[4,768,256]{2,1,0:T(8,128)(2,1)S(1)}, u32[]{:S(2)}, u32[]{:S(2)}) collective-permute-start(bf16[4,768,256]{2,1,0:T(8,128)(2,1)S(1)} %all-to-all-done.a_ref), channel_id=1, source_target_pairs={{0,1},{1,0},{2,3},{3,2},{4,5},{5,4},{6,7},{7,6},{8,9},{9,8},{10,11... | collective-permute-start | bytes 4718600 | tf_op jit(solution)/shard_map/ppermute | solution.py:334
  31.9 2.1 %copy-start.3 = (bf16[2,2048,4]{1,2,0:T(4,128)(2,1)S(1)}, bf16[2,2048,4]{1,2,0:T(4,128)(2,1)}, u32[]{:S(2)}) copy-start(bf16[2,2048,4]{1,2,0:T(4,128)(2,1)} %param.11) | copy-start | bytes 98308
  34.0 1.0 copy-start.4
  34.0 1.0 copy-start.5
  35.0 28.9 %copy-start.6 = (f32[4]{0:T(128)S(1)}, f32[4]{0:T(128)}, u32[]{:S(2)}) copy-start(f32[4]{0:T(128)} %skip_ref.1) | copy-start | bytes 52
  38.0 11.2 %copy-start.7 = (bf16[128,512]{1,0:T(8,128)(2,1)}, bf16[128,512]{1,0:T(8,128)(2,1)S(1)}, u32[]{:S(2)}) copy-start(bf16[128,512]{1,0:T(8,128)(2,1)S(1)} %get-tuple-element.31.key_ref) | copy-start | bytes 393220
  38.0 11.1 %copy-start.9 = (f32[32,512]{1,0:T(8,128)}, f32[32,512]{1,0:T(8,128)S(1)}, u32[]{:S(2)}) copy-start(f32[32,512]{1,0:T(8,128)S(1)} %get-tuple-element.33.rows_ref) | copy-start | bytes 196612
  50.0 26.4 %all-to-all-start.2 = ((bf16[8,16,384]{2,1,0:T(8,128)(2,1)}), bf16[8,16,384]{2,1,0:T(8,128)(2,1)S(1)}, u32[]{:S(2)}, u32[]{:S(2)}) async-start(bf16[8,16,384]{2,1,0:T(8,128)(2,1)} %totals.1), calls=%async_computation.2 | async-start | bytes 196608 | tf_op jit(solution)/shard_map/all_to_all | solution.py:371
  63.9 0.9 copy-start.8
  64.8 0.8 copy-start.10

commit v3 on v2

--- a/solution.py
+++ b/solution.py
@@ -17,11 +17,14 @@
 GROUP = 8
 SLICE = N // GROUP
 
-X_GROUPS = [[2 * x + c for x in range(XS)] for c in range(2)]
+X_ORDER = [3, 2, 1, 0]
+X_GROUPS = [[2 * x + c for x in X_ORDER] for c in range(2)]
 PAIRS = [[2 * x, 2 * x + 1] for x in range(XS)]
 SWAP = [(i, i ^ 1) for i in range(8)]
-NEAR = [[GROUP * g + j for j in range(GROUP)] for g in range(8)]
-FAR = [[GROUP * g + j for g in range(8)] for j in range(GROUP)]
+NEAR_ORDER = [7, 6, 5, 4, 3, 2, 1, 0]
+NEAR = [[GROUP * g + j for j in NEAR_ORDER] for g in range(8)]
+FAR_ORDER = [4, 5, 6, 7, 3, 2, 1, 0]
+FAR = [[GROUP * g + j for g in FAR_ORDER] for j in range(GROUP)]
 
 VMEM = pl.BlockSpec(memory_space=pltpu.VMEM)
 SMEM = pl.BlockSpec(memory_space=pltpu.SMEM)
@@ -62,38 +65,36 @@
     return out
 
 
-def prep_kernel(tokens_ref, bc_ref, out_ref, sems):
+def prep_kernel(tokens_ref, bc_ref, out_ref, rows_ref, sems):
     copies = []
     for x in range(XS):
-        copies.append(pltpu.make_async_copy(tokens_ref, out_ref.at[x, pl.ds(0, L)], sems.at[len(copies)]))
-        for b in range(8):
-            copies.append(
-                pltpu.make_async_copy(
-                    bc_ref.at[:, pl.ds(W * b, W)], out_ref.at[x, pl.ds(L + 32 * b, 32)], sems.at[len(copies)]
-                )
-            )
-    for copy in copies:
-        copy.start()
+        copies.append(pltpu.make_async_copy(tokens_ref, out_ref.at[x, pl.ds(0, L)], sems.at[x]))
+        copies[-1].start()
+    for b in range(8):
+        rows_ref[32 * b : 32 * (b + 1), :] = bc_ref[:, W * b : W * (b + 1)]
+    for x in range(XS):
+        copies.append(pltpu.make_async_copy(rows_ref, out_ref.at[x, pl.ds(L, W)], sems.at[XS + x]))
+        copies[-1].start()
     for copy in copies:
         copy.wait()
 
 
-def columns_kernel(core_ref, w_ref, out_ref):
-    for x in range(XS):
-        at = pl.multiple_of((2 * x + 1 - core_ref[0]) * W, W)
-        out_ref[:, W * x : W * (x + 1)] = w_ref[:, pl.ds(at, W)]
+def columns_kernel(core_ref, w_ref, own_ref, out_ref):
+    for x in range(XS):
+        for ref, c in ((own_ref, core_ref[0]), (out_ref, 1 - core_ref[0])):
+            ref[:, W * x : W * (x + 1)] = w_ref[:, pl.ds(pl.multiple_of((2 * x + c) * W, W), W)]
 
 
 def bc_columns(ref, first, j):
     row = pl.multiple_of(L + j * 32, 32)
-    return [ref[x, pl.ds(row, 32), :] for x in (first, first + 1)]
+    return [ref[X_ORDER.index(x), pl.ds(row, 32), :] for x in (first, first + 1)]
 
 
 def wide_part(ref, w_ref, c):
     total = None
     for x in range(XS):
         rows = pl.ds(pl.multiple_of((2 * x + c) * W, W), W)
-        term = dot(ref[x, 0:L, :], w_ref[rows, :])
+        term = dot(ref[X_ORDER.index(x), 0:L, :], w_ref[rows, :])
         total = term if total is None else total + term
     return total
 
@@ -105,7 +106,7 @@
         pieces = [piece for r in refs for piece in bc_columns(r, 0, j)]
         if d_ref is not None:
             pieces.append(d_ref[:, pl.ds(pl.multiple_of(j * W, W), W)])
-        term = dot(jnp.concatenate(pieces, axis=0), ref[x, 0:L, :], NT)
+        term = dot(jnp.concatenate(pieces, axis=0), ref[X_ORDER.index(x), 0:L, :], NT)
         total = term if total is None else total + term
     return total
 
@@ -114,7 +115,7 @@
     total = None
     for x in range(XS):
         pieces = [piece for r in refs for piece in bc_columns(r, 2, 2 * x + c)]
-        term = dot(ref[x, 0:L, :], jnp.concatenate(pieces, axis=0), NT)
+        term = dot(ref[X_ORDER.index(x), 0:L, :], jnp.concatenate(pieces, axis=0), NT)
         total = term if total is None else total + term
     return total
 
@@ -187,42 +188,50 @@
 
 def inner_kernel(skip_ref, query_ref, key_ref, values_ref, rows_ref, inner_ref, cols_ref):
     cols_ref[...] = jnp.concatenate([rows_ref[...], jnp.zeros((N - 32, L), F32)], axis=0).T
-    key = key_ref[...]
-    values = values_ref[...]
     tile = 128
     lane = iota((tile, W), 1) // HD
-
-    def body(i, carry):
-        at = pl.ds(pl.multiple_of(i * tile, tile), tile)
-        scores = dot(query_ref[at, :], key)
-        t = iota((tile, L), 0) + i * tile
-        s = iota((tile, L), 1)
-        lower = s < t
-        upper = s > t
-        own = values_ref[at, :].astype(F32)
-        gain = jnp.zeros((tile, W), F32)
+    gain = jnp.zeros((1, W), F32)
+    for h in range(H):
+        gain = jnp.where(iota((1, W), 1) // HD == h, skip_ref[h], gain)
+    lower = iota((tile, tile), 0) > iota((tile, tile), 1)
+    upper = iota((tile, tile), 0) < iota((tile, tile), 1)
+    for i in range(L // tile):
+        first, last = i * tile, (i + 1) * tile
+        here = slice(first, last)
+        scores = dot(query_ref[here, :], key_ref[...])
+        cols = cols_ref[here, :]
+        since = jnp.exp(cols - cols[0:1])
+        until = jnp.exp(cols[tile - 1 : tile] - cols)
+        if i > 0:
+            edge = rows_ref[0:H, first - 1 : first]
+            past = jnp.exp(edge - rows_ref[0:H, 0:first]) * rows_ref[16 : 16 + H, 0:first]
+        if last < L:
+            edge = rows_ref[H : 2 * H, last - 1 : last]
+            coming = jnp.exp(rows_ref[12 : 12 + H, last:L] - edge) * rows_ref[20 : 20 + H, last:L]
         out = jnp.zeros((tile, W), F32)
         for h in range(H):
             gap = jnp.where(
                 lower,
-                cols_ref[at, 8 + h : 9 + h] - rows_ref[h : h + 1, :],
-                rows_ref[12 + h : 13 + h, :] - cols_ref[at, H + h : H + h + 1],
+                cols[:, 8 + h : 9 + h] - rows_ref[h : h + 1, here],
+                rows_ref[12 + h : 13 + h, here] - cols[:, H + h : H + h + 1],
             )
-            step = jnp.where(lower, rows_ref[16 + h : 17 + h, :], rows_ref[20 + h : 21 + h, :])
-            weight = jnp.where(lower | upper, scores * jnp.exp(gap) * step, 0.0).astype(BF16)
-            out = jnp.where(lane == h, dot(weight, values), out)
-            gain = jnp.where(lane == h, skip_ref[h], gain)
-        inner_ref[at, :] = out + gain * own
-        return carry
-
-    lax.fori_loop(0, L // tile, body, 0)
+            step = jnp.where(lower, rows_ref[16 + h : 17 + h, here], rows_ref[20 + h : 21 + h, here])
+            own = jnp.where(lower | upper, scores[:, here] * jnp.exp(gap) * step, 0.0).astype(BF16)
+            pieces = [own]
+            if i > 0:
+                pieces.insert(0, (scores[:, 0:first] * past[h : h + 1] * since[:, 8 + h : 9 + h]).astype(BF16))
+            if last < L:
+                pieces.append((scores[:, last:L] * coming[h : h + 1] * until[:, H + h : H + h + 1]).astype(BF16))
+            out = jnp.where(lane == h, dot(jnp.concatenate(pieces, axis=1), values_ref[...]), out)
+        inner_ref[here, :] = out + gain * values_ref[here, :].astype(F32)
 
 
 def near_states(got_ref):
     extra = got_ref[:, :, 2 * W : 2 * W + N].reshape(GROUP * SLICE, N)
     decay = jnp.exp(dot(extra, spread(2 * W, 0, 2)))
-    states = [got_ref[j, :, 0 : 2 * W].astype(F32) for j in range(GROUP)]
-    decays = [decay[SLICE * j : SLICE * (j + 1)] for j in range(GROUP)]
+    order = [NEAR_ORDER.index(j) for j in range(GROUP)]
+    states = [got_ref[j, :, 0 : 2 * W].astype(F32) for j in order]
+    decays = [decay[SLICE * j : SLICE * (j + 1)] for j in order]
     return states, decays
 
 
@@ -243,7 +252,7 @@
     forward = forward.astype(BF16)
     backward = backward.astype(BF16)
     for q in range(8):
-        out_ref[q, :, 0:W] = jnp.where(q > g, forward, backward)
+        out_ref[q, :, 0:W] = jnp.where(FAR_ORDER[q] > g, forward, backward)
         out_ref[q, :, W : W + N] = log
 
 
@@ -255,21 +264,24 @@
     forward = jnp.zeros((SLICE, W), F32)
     backward = jnp.zeros((SLICE, W), F32)
     for q in range(8):
-        rows = slice(SLICE * q, SLICE * (q + 1))
-        forward = jnp.where(q < g, decay[rows, :W] * forward + far_ref[q, :, 0:W].astype(F32), forward)
+        slot = FAR_ORDER.index(q)
+        rows = slice(SLICE * slot, SLICE * (slot + 1))
+        forward = jnp.where(q < g, decay[rows, :W] * forward + far_ref[slot, :, 0:W].astype(F32), forward)
     for q in range(7, -1, -1):
-        rows = slice(SLICE * q, SLICE * (q + 1))
-        backward = jnp.where(q > g, decay[rows, W:] * backward + far_ref[q, :, 0:W].astype(F32), backward)
+        slot = FAR_ORDER.index(q)
+        rows = slice(SLICE * slot, SLICE * (slot + 1))
+        backward = jnp.where(q > g, decay[rows, W:] * backward + far_ref[slot, :, 0:W].astype(F32), backward)
     for j in range(GROUP):
-        out_ref[j, :, 0:W] = forward.astype(BF16)
+        out_ref[NEAR_ORDER.index(j), :, 0:W] = forward.astype(BF16)
         forward = decays[j][:, :W] * forward + states[j][:, :W]
     for j in range(GROUP - 1, -1, -1):
-        out_ref[j, :, W : 2 * W] = backward.astype(BF16)
+        out_ref[NEAR_ORDER.index(j), :, W : 2 * W] = backward.astype(BF16)
         backward = decays[j][:, W:] * backward + states[j][:, W:]
 
 
-def mix_kernel(inner_ref, gates_ref, query_ref, enter_ref, cols_ref, hidden_ref):
-    carried = dot(query_ref[...], enter_ref[...]) * widen(cols_ref[...], 24, 2 * W)
+def mix_kernel(inner_ref, gates_ref, query_ref, enter_ref, rows_ref, hidden_ref):
+    cols = jnp.concatenate([rows_ref[24:32], jnp.zeros((N - 8, L), F32)], axis=0).T
+    carried = dot(query_ref[...], enter_ref[...]) * widen(cols, 0, 2 * W)
     mix = inner_ref[...] + carried[:, :W] + carried[:, W:]
     gates = gates_ref[...]
     gated = mix * (gates / (1.0 + jnp.exp(-gates)))
@@ -285,8 +297,8 @@
     c = core_ref[0]
     hidden = jnp.concatenate([hidden_ref[c], hidden_ref[1 - c]], axis=1)
     for x in range(XS):
-        at = pl.ds(pl.multiple_of((2 * x + c) * W, W), W)
-        out_ref[x] = dot(hidden, jnp.concatenate([w_ref[:, at], other_ref[:, W * x : W * (x + 1)]], axis=0)).astype(BF16)
+        at = slice(W * x, W * (x + 1))
+        out_ref[X_ORDER.index(x)] = dot(hidden, jnp.concatenate([w_ref[:, at], other_ref[:, at]], axis=0)).astype(BF16)
 
 
 def sum_kernel(pieces_ref, out_ref):
@@ -295,7 +307,7 @@
     out_ref[...] = total.astype(BF16)
 
 
-def call(kernel, name, ins, outs, flops, *operands, touched=1 << 21, scratch=(), out_spec=VMEM):
+def call(kernel, name, ins, outs, flops, *operands, touched=1 << 21, scratch=(), out_spec=VMEM, limit=20 << 20):
     return pl.pallas_call(
         kernel,
         name=name,
@@ -303,7 +315,7 @@
         out_specs=[out_spec] * len(outs),
         scratch_shapes=scratch,
         out_shape=[jax.ShapeDtypeStruct(shape, kind) for shape, kind in outs],
-        compiler_params=pltpu.CompilerParams(vmem_limit_bytes=20 << 20),
+        compiler_params=pltpu.CompilerParams(vmem_limit_bytes=limit),
         cost_estimate=pl.CostEstimate(flops=flops, bytes_accessed=touched, transcendentals=1 << 16),
     )(*operands)
 
@@ -314,23 +326,26 @@
     (payload,) = call(
         prep_kernel,
         "payload",
-        [HBM, HBM],
+        [VMEM, VMEM],
         [((XS, L + W, W), BF16)],
         1,
         tokens,
         bc_weight.T,
         touched=0,
-        scratch=[pltpu.SemaphoreType.DMA((9 * XS,))],
+        scratch=[pltpu.VMEM((W, W), BF16), pltpu.SemaphoreType.DMA((2 * XS,))],
         out_spec=HBM,
+        limit=(64 << 20) - (64 << 10),
     )
     flat_weight = in_weight.reshape(D, 2 * W)
     steps_weight = dt_weight.transpose(0, 2, 1)
     mine = lax.all_to_all(payload, "tp", 0, 0, axis_index_groups=X_GROUPS, tiled=True)
-    (other_weight,) = call(
-        columns_kernel, "columns", [SMEM, VMEM], [((W, XS * W), BF16)], 1, core, out_weight
+    own_weight, other_weight = call(
+        columns_kernel, "columns", [SMEM, VMEM], [((W, XS * W), BF16)] * 2, 1, core, out_weight
     )
     other_weight = lax.ppermute(other_weight, "tp", SWAP)
-    mine, core, group, other_weight = lax.optimization_barrier((mine, core, group, other_weight))
+    mine, core, group, own_weight, other_weight = lax.optimization_barrier(
+        (mine, core, group, own_weight, other_weight)
+    )
     theirs = lax.ppermute(mine, "tp", SWAP)
     half, narrow, steps_weight = call(
         half_kernel,
@@ -357,29 +372,31 @@
         core, dt_bias, decay_rate, mine, theirs, flat_weight, steps_weight, half, narrow,
     )
     near = lax.all_to_all(message, "seq", 0, 0, axis_index_groups=NEAR, tiled=True)
-    inner, cols = call(
+    (inner,) = call(
         inner_kernel,
         "inside",
         [SMEM, VMEM, VMEM, VMEM, VMEM],
-        [((L, W), F32), ((L, N), F32)],
+        [((L, W), F32)],
         1 << 31,
         skip_gain, query, key, values, rows,
+        scratch=[pltpu.VMEM((L, N), F32)],
     )
     (totals,) = call(
         totals_kernel, "totals", [SMEM, VMEM], [((8, SLICE, W + N), BF16)], 1 << 20, group, near
     )
     far = lax.all_to_all(totals, "seq", 0, 0, axis_index_groups=FAR, tiled=True)
-    far, inner, cols = lax.optimization_barrier((far, inner, cols))
+    far, inner = lax.optimization_barrier((far, inner))
     (enters,) = call(
         enter_kernel, "enters", [SMEM, VMEM, VMEM], [((GROUP, SLICE, 2 * W), BF16)], 1 << 20, group, near, far
     )
     enter = lax.all_to_all(enters, "seq", 0, 0, axis_index_groups=NEAR, tiled=True).reshape(N, 2 * W)
     (hidden,) = call(
-        mix_kernel, "mix", [VMEM] * 5, [((L, W), BF16)], 1 << 28, inner, gates, query, enter, cols
+        mix_kernel, "mix", [VMEM] * 5, [((L, W), BF16)], 1 << 28, inner, gates, query, enter, rows
     )
     hidden = lax.all_gather(hidden, "tp", axis_index_groups=PAIRS)
     (paired,) = call(
-        pair_kernel, "pair", [SMEM, VMEM, VMEM, VMEM], [((XS, L, W), BF16)], 1 << 29, core, hidden, out_weight, other_weight
+        pair_kernel, "pair", [SMEM, VMEM, VMEM, VMEM], [((XS, L, W), BF16)], 1 << 29, core, hidden, own_weight, other_weight,
+        touched=1 << 25,
     )
     pieces = lax.all_to_all(paired, "tp", 0, 0, axis_index_groups=X_GROUPS, tiled=True)
     return call(sum_kernel, "sum", [VMEM], [((L, W), BF16)], 1 << 20, pieces)[0]

time: 112 us -> 103 us (0.920)
  waiting for transfers between devices: 14.7 us -> 7.39 us
  local copies, waits for them, and re-layouts: 5.68 us -> 3.03 us
  starting transfers between devices: 35.1 us -> 37.1 us
    all_to_all x1, waiting for transfers between devices: 7.43 us -> 0.4 us  [shards(): far = lax.all_to_all(totals, 'seq', 0, 0, axis_index_groups=FAR, tiled=True)]
    unnamed x23 -> x15, local copies, waits for them, and re-layouts: 5.68 us -> 3.03 us
    all_to_all x1, starting transfers between devices: 13.9 us -> 16.3 us  [shards(): far = lax.all_to_all(totals, 'seq', 0, 0, axis_index_groups=FAR, tiled=True)]
    all_to_all x1, starting transfers between devices: 4.99 us -> 6.99 us  [shards(): lax.all_to_all(payload, 'tp', 0, 0, axis_index_groups=X_GROUPS, tiled=True)]
    ppermute x1, starting transfers between devices: 8.69 us -> 7.38 us  [shards(): theirs = lax.ppermute(mine, 'tp', SWAP)]
where the time goes in v3:
time: 103 us; the launch traced here: 102 us
  blocking collectives  41.5 us (40%)
  starting transfers between devices  37.1 us (36%)
  Pallas kernels  13 us (13%)
  waiting for transfers between devices  7.39 us (7%)
  local copies, waits for them, and re-layouts  3.03 us (3%)
    all_to_all x1, blocking collectives, shards(): lax.all_to_all(paired, 'tp', 0, 0, axis_index_groups=X_GROUPS, tiled=True)  17.3 us
    all_to_all x1, starting transfers between devices, shards(): far = lax.all_to_all(totals, 'seq', 0, 0, axis_index_groups=FAR, tiled=True)  16.3 us
    pallas_call x10, Pallas kernels, call(): pl.pallas_call(kernel, name=name, in_specs=ins, out_specs=[out_spec] * le...  13 us
    all_to_all x1, blocking collectives, shards(): lax.all_to_all(message, 'seq', 0, 0, axis_index_groups=NEAR, tiled=True)  10.4 us
    all_to_all x1, blocking collectives, shards(): lax.all_to_all(enters, 'seq', 0, 0, axis_index_groups=NEAR, tiled=True)  7.92 us
    ppermute x1, starting transfers between devices, shards(): theirs = lax.ppermute(mine, 'tp', SWAP)  7.38 us
    all_to_all x1, starting transfers between devices, shards(): lax.all_to_all(payload, 'tp', 0, 0, axis_index_groups=X_GROUPS, tiled=True)  6.99 us
    ppermute x1, starting transfers between devices, shards(): other_weight = lax.ppermute(other_weight, 'tp', SWAP)  6.44 us
  transfers between devices with their start and end apart: 4, of which 3 were waited for; matrix products, arithmetic and copies ran while one was open for 2% of the time, Pallas kernels for 4%

profile of v3, /device:TPU:1, one launch (start us, length us, event | category | flops | bytes accessed | tf_op | source)
XLA Modules:
  0.0 102.1 jit_solution(15033033417243494371)
XLA Ops:
  0.0 2.2 %payload.1 = bf16[4,768,256]{2,1,0:T(8,128)(2,1)} custom-call(bf16[512,256]{1,0:T(8,128)(2,1)} %tokens_ref.1, bf16[32,2048]{1,0:T(8,128)(2,1)} %bitcast.14), custom_call_target="tpu_custom_call" | custom-call | flops 1 | tf_op jit(solution)/shard_map/payload/pallas_call | solution.py:311
  2.2 0.0 copy-start
  2.2 7.0 %all-to-all-start = ((bf16[4,768,256]{2,1,0:T(8,128)(2,1)}), bf16[4,768,256]{2,1,0:T(8,128)(2,1)S(1)}, u32[]{:S(2)}, u32[]{:S(2)}) async-start(bf16[4,768,256]{2,1,0:T(8,128)(2,1)} %payload.1), calls=%async_computation | async-start | bytes 3145728 | tf_op jit(solution)/shard_map/all_to_all | solution.py:341
  9.2 0.0 copy-done
  9.2 1.0 columns.1
  10.2 6.4 %collective-permute-start = (bf16[256,1024]{1,0:T(8,128)(2,1)}, bf16[256,1024]{1,0:T(8,128)(2,1)S(1)}, u32[]{:S(2)}, u32[]{:S(2)}) collective-permute-start(bf16[256,1024]{1,0:T(8,128)(2,1)} %get-tuple-element.24), channel_id=1, source_target_pairs={{0,1},{1,0},{2,3},{3,2},{4,5},{5,4},{6,7},{7,6},{8,9},{9,8},{10,11... | collective-permute-start | bytes 1572872 | tf_op jit(solution)/shard_map/ppermute | solution.py:345
  16.6 1.7 %collective-permute-done.other_ref = bf16[256,1024]{1,0:T(8,128)(2,1)S(1)} collective-permute-done((bf16[256,1024]{1,0:T(8,128)(2,1)}, bf16[256,1024]{1,0:T(8,128)(2,1)S(1)}, u32[]{:S(2)}, u32[]{:S(2)}) %collective-permute-start) | collective-permute-done | bytes 524320 | tf_op jit(solution)/shard_map/ppermute | solution.py:345
  18.4 5.3 %all-to-all-done.a_ref = bf16[4,768,256]{2,1,0:T(8,128)(2,1)S(1)} async-done(((bf16[4,768,256]{2,1,0:T(8,128)(2,1)}), bf16[4,768,256]{2,1,0:T(8,128)(2,1)S(1)}, u32[]{:S(2)}, u32[]{:S(2)}) %all-to-all-start) | async-done | bytes 1572896 | tf_op jit(solution)/shard_map/all_to_all | solution.py:341
  23.6 7.4 %collective-permute-start.1 = (bf16[4,768,256]{2,1,0:T(8,128)(2,1)S(1)}, bf16[4,768,256]{2,1,0:T(8,128)(2,1)S(1)}, u32[]{:S(2)}, u32[]{:S(2)}) collective-permute-start(bf16[4,768,256]{2,1,0:T(8,128)(2,1)S(1)} %all-to-all-done.a_ref), channel_id=1, source_target_pairs={{0,1},{1,0},{2,3},{3,2},{4,5},{5,4},{6,7},{7,6},{8,9},{9,8},{10,11... | collective-permute-start | bytes 4718600 | tf_op jit(solution)/shard_map/ppermute | solution.py:349
  31.0 0.0 copy-start.1
  31.0 2.0 %copy.9 = bf16[256,8,2,256]{3,1,2,0:T(8,128)(2,1)S(1)} copy(bf16[256,8,2,256]{3,2,1,0:T(2,128)(2,1)} %bitcast.13) | data formatting | bytes 4194304
  33.1 0.0 copy-done.1
  33.1 0.0 copy-start.2
  33.1 0.0 copy-start.3
  33.1 1.0 half.1
  34.1 0.0 collective-permute-done.1.b_ref
  34.1 0.0 copy-done.2
  34.1 0.0 copy-done.3
  34.1 0.0 copy-start.4
  34.1 3.0 %project.1 = (bf16[512,256]{1,0:T(8,128)(2,1)S(1)}, f32[512,256]{1,0:T(8,128)S(1)}, bf16[512,128]{1,0:T(8,128)(2,1)S(1)}, bf16[128,512]{1,0:T(8,128)(2,1)S(1)}, ...) custom-call(s32[1]{0:T(128)} %bitcast.1.core_ref, f32[2,4]{1,0:T(2,128)S(1)} %copy-done.2, f32[4]{0:T(128)S(1)} %copy-done.3, ...), custom_call_target="tpu_custom_call" | custom-call | flops 2147483648 | bytes 2097152 | tf_op jit(solution)/shard_map/project/pallas_call | solution.py:311
  37.1 0.0 copy-start.5
  37.1 10.4 %all_to_all.25.got_ref = bf16[8,16,640]{2,1,0:T(8,128)(2,1)S(1)} all-to-all(bf16[8,16,640]{2,1,0:T(8,128)(2,1)S(1)} %get-tuple-element.31), channel_id=1, replica_groups={{56,48,40,32,24,16,8,0},{120,112,104,96,88,80,72,64},{184,176,168,160,1..., dimensions={0} | all-to-all | bytes 327680 | tf_op jit(solution)/shard_map/all_to_all | solution.py:374
  47.5 0.0 copy-done.5
  47.5 0.8 totals.1
  48.4 16.3 %all-to-all-start.2 = ((bf16[8,16,384]{2,1,0:T(8,128)(2,1)}), bf16[8,16,384]{2,1,0:T(8,128)(2,1)S(1)}, u32[]{:S(2)}, u32[]{:S(2)}) async-start(bf16[8,16,384]{2,1,0:T(8,128)(2,1)} %totals.1), calls=%async_computation.2 | async-start | bytes 196608 | tf_op jit(solution)/shard_map/all_to_all | solution.py:387
  64.7 0.0 copy-done.4
  64.7 0.0 copy-start.6
  64.7 0.9 copy-done.6
  65.6 2.2 %inside.1.inner_ref = f32[512,256]{1,0:T(8,128)S(1)} custom-call(f32[4]{0:T(128)S(1)} %copy-done.4, bf16[512,128]{1,0:T(8,128)(2,1)S(1)} %get-tuple-element.32.query_ref, bf16[128,512]{1,0:T(8,128)(2,1)S(1)} %get-tuple-element.33.key_ref, bf16[512,256]{1,0:T(8,128)(2,1)S(1)} %copy-done.6, f32[32,512]{1,0:T(8,128)S(1)} %get-tuple-element.35.rows_ref), custom_call_target="tpu_custom_call" | custom-call | flops 2147483648 | bytes 2097152 | tf_op jit(solution)/shard_map/inside/pallas_call | solution.py:311
  67.8 0.4 all-to-all-done.2.far_ref
  68.2 0.3 enters.1
  68.5 7.9 %all_to_all.26 = bf16[8,16,512]{2,1,0:T(8,128)(2,1)S(1)} all-to-all(bf16[8,16,512]{2,1,0:T(8,128)(2,1)S(1)} %enters.1), channel_id=1, replica_groups={{56,48,40,32,24,16,8,0},{120,112,104,96,88,80,72,64},{184,176,168,160,1..., dimensions={0} | all-to-all | bytes 262144 | tf_op jit(solution)/shard_map/all_to_all | solution.py:392
  76.4 1.0 mix.1
  77.4 5.9 %all-gather = bf16[1024,256]{1,0:T(8,128)(2,1)S(1)} all-gather(bf16[512,256]{1,0:T(8,128)(2,1)S(1)} %mix.1), channel_id=2, replica_groups={{0,1},{2,3},{4,5},{6,7},{8,9},{10,11},{12,13},{14,15},{16,17},{18,19},{..., dimensions={0}, use_global_device_ids=true | all-gather | bytes 786432 | tf_op jit(solution)/shard_map/all_gather | solution.py:396
  83.3 0.7 pair.1
  84.0 17.3 %all_to_all.27.pieces_ref = bf16[4,512,256]{2,1,0:T(8,128)(2,1)S(1)} all-to-all(bf16[4,512,256]{2,1,0:T(8,128)(2,1)S(1)} %pair.1), channel_id=1, replica_groups={{6,4,2,0},{7,5,3,1},{14,12,10,8},{15,13,11,9},{22,20,18,16},{23,21,19,1..., dimensions={0} | all-to-all | bytes 2097152 | tf_op jit(solution)/shard_map/all_to_all | solution.py:401
  101.2 0.8 sum.1
Async XLA Ops:
  2.2 7.0 %copy-start = (bf16[256,2048]{1,0:T(8,128)(2,1)S(1)}, bf16[256,2048]{1,0:T(8,128)(2,1)}, u32[]{:S(2)}) copy-start(bf16[256,2048]{1,0:T(8,128)(2,1)} %w_ref.1) | copy-start | bytes 3145732
  2.2 21.4 %all-to-all-start = ((bf16[4,768,256]{2,1,0:T(8,128)(2,1)}), bf16[4,768,256]{2,1,0:T(8,128)(2,1)S(1)}, u32[]{:S(2)}, u32[]{:S(2)}) async-start(bf16[4,768,256]{2,1,0:T(8,128)(2,1)} %payload.1), calls=%async_computation | async-start | bytes 3145728 | tf_op jit(solution)/shard_map/all_to_all | solution.py:341
  10.2 8.2 %collective-permute-start = (bf16[256,1024]{1,0:T(8,128)(2,1)}, bf16[256,1024]{1,0:T(8,128)(2,1)S(1)}, u32[]{:S(2)}, u32[]{:S(2)}) collective-permute-start(bf16[256,1024]{1,0:T(8,128)(2,1)} %get-tuple-element.24), channel_id=1, source_target_pairs={{0,1},{1,0},{2,3},{3,2},{4,5},{5,4},{6,7},{7,6},{8,9},{9,8},{10,11... | collective-permute-start | bytes 1572872 | tf_op jit(solution)/shard_map/ppermute | solution.py:345
  23.6 10.5 %collective-permute-start.1 = (bf16[4,768,256]{2,1,0:T(8,128)(2,1)S(1)}, bf16[4,768,256]{2,1,0:T(8,128)(2,1)S(1)}, u32[]{:S(2)}, u32[]{:S(2)}) collective-permute-start(bf16[4,768,256]{2,1,0:T(8,128)(2,1)S(1)} %all-to-all-done.a_ref), channel_id=1, source_target_pairs={{0,1},{1,0},{2,3},{3,2},{4,5},{5,4},{6,7},{7,6},{8,9},{9,8},{10,11... | collective-permute-start | bytes 4718600 | tf_op jit(solution)/shard_map/ppermute | solution.py:349
  31.0 2.1 %copy-start.1 = (bf16[2,2048,4]{1,2,0:T(4,128)(2,1)S(1)}, bf16[2,2048,4]{1,2,0:T(4,128)(2,1)}, u32[]{:S(2)}) copy-start(bf16[2,2048,4]{1,2,0:T(4,128)(2,1)} %param.11) | copy-start | bytes 98308
  33.1 1.0 copy-start.2
  33.1 1.0 copy-start.3
  34.1 30.6 %copy-start.4 = (f32[4]{0:T(128)S(1)}, f32[4]{0:T(128)}, u32[]{:S(2)}) copy-start(f32[4]{0:T(128)} %skip_ref.1) | copy-start | bytes 52
  37.1 10.4 %copy-start.5 = (bf16[512,256]{1,0:T(8,128)(2,1)}, bf16[512,256]{1,0:T(8,128)(2,1)S(1)}, u32[]{:S(2)}) copy-start(bf16[512,256]{1,0:T(8,128)(2,1)S(1)} %get-tuple-element.34.values_ref) | copy-start | bytes 786436
  48.4 19.8 %all-to-all-start.2 = ((bf16[8,16,384]{2,1,0:T(8,128)(2,1)}), bf16[8,16,384]{2,1,0:T(8,128)(2,1)S(1)}, u32[]{:S(2)}, u32[]{:S(2)}) async-start(bf16[8,16,384]{2,1,0:T(8,128)(2,1)} %totals.1), calls=%async_computation.2 | async-start | bytes 196608 | tf_op jit(solution)/shard_map/all_to_all | solution.py:387
  64.7 1.0 copy-start.6

commit v4 on v3

--- a/solution.py
+++ b/solution.py
@@ -17,13 +17,15 @@
 GROUP = 8
 SLICE = N // GROUP
 
-X_ORDER = [3, 2, 1, 0]
+X_ORDER = [2, 3, 1, 0]
 X_GROUPS = [[2 * x + c for x in X_ORDER] for c in range(2)]
+SUM_ORDER = [2, 3, 1, 0]
+SUM_GROUPS = [[2 * x + c for x in SUM_ORDER] for c in range(2)]
 PAIRS = [[2 * x, 2 * x + 1] for x in range(XS)]
 SWAP = [(i, i ^ 1) for i in range(8)]
-NEAR_ORDER = [7, 6, 5, 4, 3, 2, 1, 0]
+NEAR_ORDER = [6, 7, 5, 4, 3, 2, 1, 0]
 NEAR = [[GROUP * g + j for j in NEAR_ORDER] for g in range(8)]
-FAR_ORDER = [4, 5, 6, 7, 3, 2, 1, 0]
+FAR_ORDER = [5, 4, 6, 7, 3, 2, 1, 0]
 FAR = [[GROUP * g + j for g in FAR_ORDER] for j in range(GROUP)]
 
 VMEM = pl.BlockSpec(memory_space=pltpu.VMEM)
@@ -298,7 +300,7 @@
     hidden = jnp.concatenate([hidden_ref[c], hidden_ref[1 - c]], axis=1)
     for x in range(XS):
         at = slice(W * x, W * (x + 1))
-        out_ref[X_ORDER.index(x)] = dot(hidden, jnp.concatenate([w_ref[:, at], other_ref[:, at]], axis=0)).astype(BF16)
+        out_ref[SUM_ORDER.index(x)] = dot(hidden, jnp.concatenate([w_ref[:, at], other_ref[:, at]], axis=0)).astype(BF16)
 
 
 def sum_kernel(pieces_ref, out_ref):
@@ -398,7 +400,7 @@
         pair_kernel, "pair", [SMEM, VMEM, VMEM, VMEM], [((XS, L, W), BF16)], 1 << 29, core, hidden, own_weight, other_weight,
         touched=1 << 25,
     )
-    pieces = lax.all_to_all(paired, "tp", 0, 0, axis_index_groups=X_GROUPS, tiled=True)
+    pieces = lax.all_to_all(paired, "tp", 0, 0, axis_index_groups=SUM_GROUPS, tiled=True)
     return call(sum_kernel, "sum", [VMEM], [((L, W), BF16)], 1 << 20, pieces)[0]
 
 

time: 103 us -> 100 us (0.971)
  blocking collectives: 41.5 us -> 40 us
    all_to_all x1, starting transfers between devices: 16.3 us -> 15.1 us  [shards(): far = lax.all_to_all(totals, 'seq', 0, 0, axis_index_groups=FAR, tiled=True)]
where the time goes in v4:
time: 100 us; the launch traced here: 99.6 us
  blocking collectives  40 us (40%)
  starting transfers between devices  36.2 us (36%)
  Pallas kernels  13 us (13%)
  waiting for transfers between devices  7.25 us (7%)
  local copies, waits for them, and re-layouts  3.03 us (3%)
    all_to_all x1, blocking collectives, shards(): lax.all_to_all(paired, 'tp', 0, 0, axis_index_groups=SUM_GROUPS, tiled=True)  16.5 us
    all_to_all x1, starting transfers between devices, shards(): far = lax.all_to_all(totals, 'seq', 0, 0, axis_index_groups=FAR, tiled=True)  15.1 us
    pallas_call x10, Pallas kernels, call(): pl.pallas_call(kernel, name=name, in_specs=ins, out_specs=[out_spec] * le...  13 us
    all_to_all x1, blocking collectives, shards(): lax.all_to_all(message, 'seq', 0, 0, axis_index_groups=NEAR, tiled=True)  9.43 us
    all_to_all x1, blocking collectives, shards(): lax.all_to_all(enters, 'seq', 0, 0, axis_index_groups=NEAR, tiled=True)  8.23 us
    ppermute x1, starting transfers between devices, shards(): theirs = lax.ppermute(mine, 'tp', SWAP)  7.38 us
    all_to_all x1, starting transfers between devices, shards(): lax.all_to_all(payload, 'tp', 0, 0, axis_index_groups=X_GROUPS, tiled=True)  7.25 us
    ppermute x1, starting transfers between devices, shards(): other_weight = lax.ppermute(other_weight, 'tp', SWAP)  6.46 us
  transfers between devices with their start and end apart: 4, of which 3 were waited for; matrix products, arithmetic and copies ran while one was open for 2% of the time, Pallas kernels for 4%

profile of v4, /device:TPU:1, one launch (start us, length us, event | category | flops | bytes accessed | tf_op | source)
XLA Modules:
  0.0 99.6 jit_solution(14975936656311114271)
XLA Ops:
  0.0 2.2 %payload.1 = bf16[4,768,256]{2,1,0:T(8,128)(2,1)} custom-call(bf16[512,256]{1,0:T(8,128)(2,1)} %tokens_ref.1, bf16[32,2048]{1,0:T(8,128)(2,1)} %bitcast.14), custom_call_target="tpu_custom_call" | custom-call | flops 1 | tf_op jit(solution)/shard_map/payload/pallas_call | solution.py:313
  2.2 0.0 copy-start
  2.2 7.3 %all-to-all-start = ((bf16[4,768,256]{2,1,0:T(8,128)(2,1)}), bf16[4,768,256]{2,1,0:T(8,128)(2,1)S(1)}, u32[]{:S(2)}, u32[]{:S(2)}) async-start(bf16[4,768,256]{2,1,0:T(8,128)(2,1)} %payload.1), calls=%async_computation | async-start | bytes 3145728 | tf_op jit(solution)/shard_map/all_to_all | solution.py:343
  9.5 0.0 copy-done
  9.5 1.0 columns.1
  10.4 6.5 %collective-permute-start = (bf16[256,1024]{1,0:T(8,128)(2,1)}, bf16[256,1024]{1,0:T(8,128)(2,1)S(1)}, u32[]{:S(2)}, u32[]{:S(2)}) collective-permute-start(bf16[256,1024]{1,0:T(8,128)(2,1)} %get-tuple-element.24), channel_id=1, source_target_pairs={{0,1},{1,0},{2,3},{3,2},{4,5},{5,4},{6,7},{7,6},{8,9},{9,8},{10,11... | collective-permute-start | bytes 1572872 | tf_op jit(solution)/shard_map/ppermute | solution.py:347
  16.9 1.7 %collective-permute-done.other_ref = bf16[256,1024]{1,0:T(8,128)(2,1)S(1)} collective-permute-done((bf16[256,1024]{1,0:T(8,128)(2,1)}, bf16[256,1024]{1,0:T(8,128)(2,1)S(1)}, u32[]{:S(2)}, u32[]{:S(2)}) %collective-permute-start) | collective-permute-done | bytes 524320 | tf_op jit(solution)/shard_map/ppermute | solution.py:347
  18.6 4.3 %all-to-all-done.a_ref = bf16[4,768,256]{2,1,0:T(8,128)(2,1)S(1)} async-done(((bf16[4,768,256]{2,1,0:T(8,128)(2,1)}), bf16[4,768,256]{2,1,0:T(8,128)(2,1)S(1)}, u32[]{:S(2)}, u32[]{:S(2)}) %all-to-all-start) | async-done | bytes 1572896 | tf_op jit(solution)/shard_map/all_to_all | solution.py:343
  23.0 7.4 %collective-permute-start.1 = (bf16[4,768,256]{2,1,0:T(8,128)(2,1)S(1)}, bf16[4,768,256]{2,1,0:T(8,128)(2,1)S(1)}, u32[]{:S(2)}, u32[]{:S(2)}) collective-permute-start(bf16[4,768,256]{2,1,0:T(8,128)(2,1)S(1)} %all-to-all-done.a_ref), channel_id=1, source_target_pairs={{0,1},{1,0},{2,3},{3,2},{4,5},{5,4},{6,7},{7,6},{8,9},{9,8},{10,11... | collective-permute-start | bytes 4718600 | tf_op jit(solution)/shard_map/ppermute | solution.py:351
  30.4 0.0 copy-start.1
  30.4 2.0 %copy.9 = bf16[256,8,2,256]{3,1,2,0:T(8,128)(2,1)S(1)} copy(bf16[256,8,2,256]{3,2,1,0:T(2,128)(2,1)} %bitcast.13) | data formatting | bytes 4194304
  32.4 0.0 copy-done.1
  32.4 0.0 copy-start.2
  32.5 0.0 copy-start.3
  32.5 1.0 half.1
  33.4 0.0 collective-permute-done.1.b_ref
  33.4 0.0 copy-done.2
  33.5 0.0 copy-done.3
  33.5 0.0 copy-start.4
  33.5 3.0 %project.1 = (bf16[512,256]{1,0:T(8,128)(2,1)S(1)}, f32[512,256]{1,0:T(8,128)S(1)}, bf16[512,128]{1,0:T(8,128)(2,1)S(1)}, bf16[128,512]{1,0:T(8,128)(2,1)S(1)}, ...) custom-call(s32[1]{0:T(128)} %bitcast.1.core_ref, f32[2,4]{1,0:T(2,128)S(1)} %copy-done.2, f32[4]{0:T(128)S(1)} %copy-done.3, ...), custom_call_target="tpu_custom_call" | custom-call | flops 2147483648 | bytes 2097152 | tf_op jit(solution)/shard_map/project/pallas_call | solution.py:313
  36.5 0.0 copy-start.5
  36.5 9.4 %all_to_all.25.got_ref = bf16[8,16,640]{2,1,0:T(8,128)(2,1)S(1)} all-to-all(bf16[8,16,640]{2,1,0:T(8,128)(2,1)S(1)} %get-tuple-element.31), channel_id=1, replica_groups={{48,56,40,32,24,16,8,0},{112,120,104,96,88,80,72,64},{176,184,168,160,1..., dimensions={0} | all-to-all | bytes 327680 | tf_op jit(solution)/shard_map/all_to_all | solution.py:376
  45.9 0.0 copy-done.5
  45.9 0.8 totals.1
  46.8 15.1 %all-to-all-start.2 = ((bf16[8,16,384]{2,1,0:T(8,128)(2,1)}), bf16[8,16,384]{2,1,0:T(8,128)(2,1)S(1)}, u32[]{:S(2)}, u32[]{:S(2)}) async-start(bf16[8,16,384]{2,1,0:T(8,128)(2,1)} %totals.1), calls=%async_computation.2 | async-start | bytes 196608 | tf_op jit(solution)/shard_map/all_to_all | solution.py:389
  61.9 0.0 copy-done.4
  61.9 0.0 copy-start.6
  61.9 0.9 copy-done.6
  62.8 2.2 %inside.1.inner_ref = f32[512,256]{1,0:T(8,128)S(1)} custom-call(f32[4]{0:T(128)S(1)} %copy-done.4, bf16[512,128]{1,0:T(8,128)(2,1)S(1)} %get-tuple-element.32.query_ref, bf16[128,512]{1,0:T(8,128)(2,1)S(1)} %get-tuple-element.33.key_ref, bf16[512,256]{1,0:T(8,128)(2,1)S(1)} %copy-done.6, f32[32,512]{1,0:T(8,128)S(1)} %get-tuple-element.35.rows_ref), custom_call_target="tpu_custom_call" | custom-call | flops 2147483648 | bytes 2097152 | tf_op jit(solution)/shard_map/inside/pallas_call | solution.py:313
  65.0 1.2 %all-to-all-done.2.far_ref = bf16[8,16,384]{2,1,0:T(8,128)(2,1)S(1)} async-done(((bf16[8,16,384]{2,1,0:T(8,128)(2,1)}), bf16[8,16,384]{2,1,0:T(8,128)(2,1)S(1)}, u32[]{:S(2)}, u32[]{:S(2)}) %all-to-all-start.2) | async-done | bytes 98336 | tf_op jit(solution)/shard_map/all_to_all | solution.py:389
  66.2 0.3 enters.1
  66.5 8.2 %all_to_all.26 = bf16[8,16,512]{2,1,0:T(8,128)(2,1)S(1)} all-to-all(bf16[8,16,512]{2,1,0:T(8,128)(2,1)S(1)} %enters.1), channel_id=1, replica_groups={{48,56,40,32,24,16,8,0},{112,120,104,96,88,80,72,64},{176,184,168,160,1..., dimensions={0} | all-to-all | bytes 262144 | tf_op jit(solution)/shard_map/all_to_all | solution.py:394
  74.7 1.0 mix.1
  75.7 5.8 %all-gather = bf16[1024,256]{1,0:T(8,128)(2,1)S(1)} all-gather(bf16[512,256]{1,0:T(8,128)(2,1)S(1)} %mix.1), channel_id=2, replica_groups={{0,1},{2,3},{4,5},{6,7},{8,9},{10,11},{12,13},{14,15},{16,17},{18,19},{..., dimensions={0}, use_global_device_ids=true | all-gather | bytes 786432 | tf_op jit(solution)/shard_map/all_gather | solution.py:398
  81.5 0.7 pair.1
  82.2 16.5 %all_to_all.27.pieces_ref = bf16[4,512,256]{2,1,0:T(8,128)(2,1)S(1)} all-to-all(bf16[4,512,256]{2,1,0:T(8,128)(2,1)S(1)} %pair.1), channel_id=1, replica_groups={{4,6,2,0},{5,7,3,1},{12,14,10,8},{13,15,11,9},{20,22,18,16},{21,23,19,1..., dimensions={0} | all-to-all | bytes 2097152 | tf_op jit(solution)/shard_map/all_to_all | solution.py:403
  98.7 0.8 sum.1
Async XLA Ops:
  2.2 7.3 %copy-start = (bf16[256,2048]{1,0:T(8,128)(2,1)S(1)}, bf16[256,2048]{1,0:T(8,128)(2,1)}, u32[]{:S(2)}) copy-start(bf16[256,2048]{1,0:T(8,128)(2,1)} %w_ref.1) | copy-start | bytes 3145732
  2.2 20.8 %all-to-all-start = ((bf16[4,768,256]{2,1,0:T(8,128)(2,1)}), bf16[4,768,256]{2,1,0:T(8,128)(2,1)S(1)}, u32[]{:S(2)}, u32[]{:S(2)}) async-start(bf16[4,768,256]{2,1,0:T(8,128)(2,1)} %payload.1), calls=%async_computation | async-start | bytes 3145728 | tf_op jit(solution)/shard_map/all_to_all | solution.py:343
  10.4 8.2 %collective-permute-start = (bf16[256,1024]{1,0:T(8,128)(2,1)}, bf16[256,1024]{1,0:T(8,128)(2,1)S(1)}, u32[]{:S(2)}, u32[]{:S(2)}) collective-permute-start(bf16[256,1024]{1,0:T(8,128)(2,1)} %get-tuple-element.24), channel_id=1, source_target_pairs={{0,1},{1,0},{2,3},{3,2},{4,5},{5,4},{6,7},{7,6},{8,9},{9,8},{10,11... | collective-permute-start | bytes 1572872 | tf_op jit(solution)/shard_map/ppermute | solution.py:347
  23.0 10.5 %collective-permute-start.1 = (bf16[4,768,256]{2,1,0:T(8,128)(2,1)S(1)}, bf16[4,768,256]{2,1,0:T(8,128)(2,1)S(1)}, u32[]{:S(2)}, u32[]{:S(2)}) collective-permute-start(bf16[4,768,256]{2,1,0:T(8,128)(2,1)S(1)} %all-to-all-done.a_ref), channel_id=1, source_target_pairs={{0,1},{1,0},{2,3},{3,2},{4,5},{5,4},{6,7},{7,6},{8,9},{9,8},{10,11... | collective-permute-start | bytes 4718600 | tf_op jit(solution)/shard_map/ppermute | solution.py:351
  30.4 2.1 %copy-start.1 = (bf16[2,2048,4]{1,2,0:T(4,128)(2,1)S(1)}, bf16[2,2048,4]{1,2,0:T(4,128)(2,1)}, u32[]{:S(2)}) copy-start(bf16[2,2048,4]{1,2,0:T(4,128)(2,1)} %param.11) | copy-start | bytes 98308
  32.4 1.0 %copy-start.2 = (f32[2,4]{1,0:T(2,128)S(1)}, f32[2,4]{1,0:T(2,128)}, u32[]{:S(2)}) copy-start(f32[2,4]{1,0:T(2,128)} %bias_ref.1) | copy-start | bytes 100
  32.5 1.0 %copy-start.3 = (f32[4]{0:T(128)S(1)}, f32[4]{0:T(128)}, u32[]{:S(2)}) copy-start(f32[4]{0:T(128)} %rate_ref.1) | copy-start | bytes 52
  33.5 28.4 %copy-start.4 = (f32[4]{0:T(128)S(1)}, f32[4]{0:T(128)}, u32[]{:S(2)}) copy-start(f32[4]{0:T(128)} %skip_ref.1) | copy-start | bytes 52
  36.5 9.4 %copy-start.5 = (bf16[512,256]{1,0:T(8,128)(2,1)}, bf16[512,256]{1,0:T(8,128)(2,1)S(1)}, u32[]{:S(2)}) copy-start(bf16[512,256]{1,0:T(8,128)(2,1)S(1)} %get-tuple-element.34.values_ref) | copy-start | bytes 786436
  46.8 19.4 %all-to-all-start.2 = ((bf16[8,16,384]{2,1,0:T(8,128)(2,1)}), bf16[8,16,384]{2,1,0:T(8,128)(2,1)S(1)}, u32[]{:S(2)}, u32[]{:S(2)}) async-start(bf16[8,16,384]{2,1,0:T(8,128)(2,1)} %totals.1), calls=%async_computation.2 | async-start | bytes 196608 | tf_op jit(solution)/shard_map/all_to_all | solution.py:389
  61.9 1.0 copy-start.6

commit v5 on v4

--- a/solution.py
+++ b/solution.py
@@ -105,19 +105,10 @@
     total = None
     for x in range(XS):
         j = 2 * x + c
-        pieces = [piece for r in refs for piece in bc_columns(r, 0, j)]
+        pieces = [piece for first in (0, 2) for r in refs for piece in bc_columns(r, first, j)]
         if d_ref is not None:
             pieces.append(d_ref[:, pl.ds(pl.multiple_of(j * W, W), W)])
         term = dot(jnp.concatenate(pieces, axis=0), ref[X_ORDER.index(x), 0:L, :], NT)
-        total = term if total is None else total + term
-    return total
-
-
-def query_part(ref, refs, c):
-    total = None
-    for x in range(XS):
-        pieces = [piece for r in refs for piece in bc_columns(r, 2, 2 * x + c)]
-        term = dot(ref[X_ORDER.index(x), 0:L, :], jnp.concatenate(pieces, axis=0), NT)
         total = term if total is None else total + term
     return total
 
@@ -139,16 +130,16 @@
     c = core_ref[0]
     later = narrow_part(b_ref, (a_ref, b_ref), d_ref, 1 - c)
     earlier = narrow_ref[...]
-    key = jnp.concatenate(
-        [earlier[0:64] + later[0:64], narrow_part(a_ref, (b_ref,), None, c) + later[64:128]], axis=0
-    ).astype(BF16)
+    crossed = narrow_part(a_ref, (b_ref,), None, c)
+    key = jnp.concatenate([earlier[0:64] + later[0:64], crossed[0:64] + later[64:128]], axis=0).astype(BF16)
     key_ref[...] = key
+    query = jnp.concatenate([earlier[64:128] + later[128:192], crossed[64:128] + later[192:256]], axis=0)
+    query_ref[...] = query.T.astype(BF16)
     both = half_ref[...] + wide_part(b_ref, w_ref, 1 - c)
+    gates_ref[...] = both[:, W:]
     values = both[:, :W].astype(BF16)
     values_ref[...] = values
-    gates_ref[...] = both[:, W:]
-    query_ref[...] = (query_part(a_ref, (a_ref, b_ref), c) + query_part(b_ref, (a_ref, b_ref), 1 - c)).astype(BF16)
-    raw = (earlier[64:72] + later[128:136]) + column(bias_ref, lambda r, i: r[i // H, i % H])
+    raw = (earlier[128:136] + later[256:264]) + column(bias_ref, lambda r, i: r[i // H, i % H])
     steps = jnp.maximum(raw, 0.0) + jnp.log1p(jnp.exp(-jnp.abs(raw)))
     logs = -column(rate_ref, lambda r, i: r[i % H]) * steps
     p1 = logs.astype(BF16)
@@ -353,7 +344,7 @@
         half_kernel,
         "half",
         [SMEM, VMEM, VMEM, VMEM],
-        [((L, 2 * W), F32), ((80, L), F32), ((SLICE, D), BF16)],
+        [((L, 2 * W), F32), ((144, L), F32), ((SLICE, D), BF16)],
         1 << 30,
         core, mine, flat_weight, steps_weight,
         scratch=[pltpu.VMEM((SLICE, D), F32)],

time: 100 us -> 99.5 us (level)
  no operation moved by 1% of the time
where the time goes in v5:
time: 99.5 us; the launch traced here: 99 us
  blocking collectives  40 us (40%)
  starting transfers between devices  36.1 us (36%)
  Pallas kernels  12.4 us (12%)
  waiting for transfers between devices  7.25 us (7%)
  local copies, waits for them, and re-layouts  3.03 us (3%)
    all_to_all x1, blocking collectives, shards(): lax.all_to_all(paired, 'tp', 0, 0, axis_index_groups=SUM_GROUPS, tiled=True)  16.5 us
    all_to_all x1, starting transfers between devices, shards(): far = lax.all_to_all(totals, 'seq', 0, 0, axis_index_groups=FAR, tiled=True)  15 us
    pallas_call x10, Pallas kernels, call(): pl.pallas_call(kernel, name=name, in_specs=ins, out_specs=[out_spec] * le...  12.4 us
    all_to_all x1, blocking collectives, shards(): lax.all_to_all(message, 'seq', 0, 0, axis_index_groups=NEAR, tiled=True)  9.5 us
    all_to_all x1, blocking collectives, shards(): lax.all_to_all(enters, 'seq', 0, 0, axis_index_groups=NEAR, tiled=True)  8.23 us
    ppermute x1, starting transfers between devices, shards(): theirs = lax.ppermute(mine, 'tp', SWAP)  7.38 us
    all_to_all x1, starting transfers between devices, shards(): lax.all_to_all(payload, 'tp', 0, 0, axis_index_groups=X_GROUPS, tiled=True)  7.25 us
    ppermute x1, starting transfers between devices, shards(): other_weight = lax.ppermute(other_weight, 'tp', SWAP)  6.46 us
  transfers between devices with their start and end apart: 4, of which 3 were waited for; matrix products, arithmetic and copies ran while one was open for 2% of the time, Pallas kernels for 4%

profile of v5, /device:TPU:1, one launch (start us, length us, event | category | flops | bytes accessed | tf_op | source)
XLA Modules:
  0.0 99.0 jit_solution(12447198957602708360)
XLA Ops:
  0.0 2.2 %payload.1 = bf16[4,768,256]{2,1,0:T(8,128)(2,1)} custom-call(bf16[512,256]{1,0:T(8,128)(2,1)} %tokens_ref.1, bf16[32,2048]{1,0:T(8,128)(2,1)} %bitcast.14), custom_call_target="tpu_custom_call" | custom-call | flops 1 | tf_op jit(solution)/shard_map/payload/pallas_call | solution.py:304
  2.2 0.0 copy-start
  2.2 7.3 %all-to-all-start = ((bf16[4,768,256]{2,1,0:T(8,128)(2,1)}), bf16[4,768,256]{2,1,0:T(8,128)(2,1)S(1)}, u32[]{:S(2)}, u32[]{:S(2)}) async-start(bf16[4,768,256]{2,1,0:T(8,128)(2,1)} %payload.1), calls=%async_computation | async-start | bytes 3145728 | tf_op jit(solution)/shard_map/all_to_all | solution.py:334
  9.5 0.0 copy-done
  9.5 1.0 columns.1
  10.4 6.5 %collective-permute-start = (bf16[256,1024]{1,0:T(8,128)(2,1)}, bf16[256,1024]{1,0:T(8,128)(2,1)S(1)}, u32[]{:S(2)}, u32[]{:S(2)}) collective-permute-start(bf16[256,1024]{1,0:T(8,128)(2,1)} %get-tuple-element.24), channel_id=1, source_target_pairs={{0,1},{1,0},{2,3},{3,2},{4,5},{5,4},{6,7},{7,6},{8,9},{9,8},{10,11... | collective-permute-start | bytes 1572872 | tf_op jit(solution)/shard_map/ppermute | solution.py:338
  16.9 1.7 %collective-permute-done.other_ref = bf16[256,1024]{1,0:T(8,128)(2,1)S(1)} collective-permute-done((bf16[256,1024]{1,0:T(8,128)(2,1)}, bf16[256,1024]{1,0:T(8,128)(2,1)S(1)}, u32[]{:S(2)}, u32[]{:S(2)}) %collective-permute-start) | collective-permute-done | bytes 524320 | tf_op jit(solution)/shard_map/ppermute | solution.py:338
  18.6 4.3 %all-to-all-done.a_ref = bf16[4,768,256]{2,1,0:T(8,128)(2,1)S(1)} async-done(((bf16[4,768,256]{2,1,0:T(8,128)(2,1)}), bf16[4,768,256]{2,1,0:T(8,128)(2,1)S(1)}, u32[]{:S(2)}, u32[]{:S(2)}) %all-to-all-start) | async-done | bytes 1572896 | tf_op jit(solution)/shard_map/all_to_all | solution.py:334
  23.0 7.4 %collective-permute-start.1 = (bf16[4,768,256]{2,1,0:T(8,128)(2,1)S(1)}, bf16[4,768,256]{2,1,0:T(8,128)(2,1)S(1)}, u32[]{:S(2)}, u32[]{:S(2)}) collective-permute-start(bf16[4,768,256]{2,1,0:T(8,128)(2,1)S(1)} %all-to-all-done.a_ref), channel_id=1, source_target_pairs={{0,1},{1,0},{2,3},{3,2},{4,5},{5,4},{6,7},{7,6},{8,9},{9,8},{10,11... | collective-permute-start | bytes 4718600 | tf_op jit(solution)/shard_map/ppermute | solution.py:342
  30.4 0.0 copy-start.1
  30.4 2.0 %copy.9 = bf16[256,8,2,256]{3,1,2,0:T(8,128)(2,1)S(1)} copy(bf16[256,8,2,256]{3,2,1,0:T(2,128)(2,1)} %bitcast.13) | data formatting | bytes 4194304
  32.4 0.0 copy-done.1
  32.4 0.0 copy-start.2
  32.5 0.0 copy-start.3
  32.5 1.0 %half.1 = (f32[512,512]{1,0:T(8,128)S(1)}, f32[144,512]{1,0:T(8,128)S(1)}, bf16[16,2048]{1,0:T(8,128)(2,1)S(1)}) custom-call(s32[1]{0:T(128)} %bitcast.1.core_ref, bf16[4,768,256]{2,1,0:T(8,128)(2,1)S(1)} %all-to-all-done.a_ref, bf16[2048,512]{1,0:T(8,128)(2,1)S(1)} %bitcast.8, bf16[2,4,2048]{2,1,0:T(4,128)(2,1)S(1)} %bitcast.12), custom_call_target="tpu_custom_call" | custom-call | flops 1073741824 | bytes 2097152 | tf_op jit(solution)/shard_map/half/pallas_call | solution.py:304
  33.5 0.0 collective-permute-done.1.b_ref
  33.5 0.0 copy-done.2
  33.5 0.0 copy-done.3
  33.5 0.0 copy-start.4
  33.5 2.4 %project.1 = (bf16[512,256]{1,0:T(8,128)(2,1)S(1)}, f32[512,256]{1,0:T(8,128)S(1)}, bf16[512,128]{1,0:T(8,128)(2,1)S(1)}, bf16[128,512]{1,0:T(8,128)(2,1)S(1)}, ...) custom-call(s32[1]{0:T(128)} %bitcast.1.core_ref, f32[2,4]{1,0:T(2,128)S(1)} %copy-done.2, f32[4]{0:T(128)S(1)} %copy-done.3, ...), custom_call_target="tpu_custom_call" | custom-call | flops 2147483648 | bytes 2097152 | tf_op jit(solution)/shard_map/project/pallas_call | solution.py:304
  36.0 0.0 copy-start.5
  36.0 9.5 %all_to_all.25.got_ref = bf16[8,16,640]{2,1,0:T(8,128)(2,1)S(1)} all-to-all(bf16[8,16,640]{2,1,0:T(8,128)(2,1)S(1)} %get-tuple-element.31), channel_id=1, replica_groups={{48,56,40,32,24,16,8,0},{112,120,104,96,88,80,72,64},{176,184,168,160,1..., dimensions={0} | all-to-all | bytes 327680 | tf_op jit(solution)/shard_map/all_to_all | solution.py:367
  45.5 0.0 copy-done.5
  45.5 0.8 totals.1
  46.3 15.0 %all-to-all-start.2 = ((bf16[8,16,384]{2,1,0:T(8,128)(2,1)}), bf16[8,16,384]{2,1,0:T(8,128)(2,1)S(1)}, u32[]{:S(2)}, u32[]{:S(2)}) async-start(bf16[8,16,384]{2,1,0:T(8,128)(2,1)} %totals.1), calls=%async_computation.2 | async-start | bytes 196608 | tf_op jit(solution)/shard_map/all_to_all | solution.py:380
  61.4 0.0 copy-done.4
  61.4 0.0 copy-start.6
  61.4 0.9 copy-done.6
  62.3 2.2 %inside.1.inner_ref = f32[512,256]{1,0:T(8,128)S(1)} custom-call(f32[4]{0:T(128)S(1)} %copy-done.4, bf16[512,128]{1,0:T(8,128)(2,1)S(1)} %get-tuple-element.32.query_ref, bf16[128,512]{1,0:T(8,128)(2,1)S(1)} %get-tuple-element.33.key_ref, bf16[512,256]{1,0:T(8,128)(2,1)S(1)} %copy-done.6, f32[32,512]{1,0:T(8,128)S(1)} %get-tuple-element.35.rows_ref), custom_call_target="tpu_custom_call" | custom-call | flops 2147483648 | bytes 2097152 | tf_op jit(solution)/shard_map/inside/pallas_call | solution.py:304
  64.5 1.2 %all-to-all-done.2.far_ref = bf16[8,16,384]{2,1,0:T(8,128)(2,1)S(1)} async-done(((bf16[8,16,384]{2,1,0:T(8,128)(2,1)}), bf16[8,16,384]{2,1,0:T(8,128)(2,1)S(1)}, u32[]{:S(2)}, u32[]{:S(2)}) %all-to-all-start.2) | async-done | bytes 98336 | tf_op jit(solution)/shard_map/all_to_all | solution.py:380
  65.7 0.3 enters.1
  66.0 8.2 %all_to_all.26 = bf16[8,16,512]{2,1,0:T(8,128)(2,1)S(1)} all-to-all(bf16[8,16,512]{2,1,0:T(8,128)(2,1)S(1)} %enters.1), channel_id=1, replica_groups={{48,56,40,32,24,16,8,0},{112,120,104,96,88,80,72,64},{176,184,168,160,1..., dimensions={0} | all-to-all | bytes 262144 | tf_op jit(solution)/shard_map/all_to_all | solution.py:385
  74.2 1.0 %mix.1 = bf16[512,256]{1,0:T(8,128)(2,1)S(1)} custom-call(f32[512,256]{1,0:T(8,128)S(1)} %inside.1.inner_ref, f32[512,256]{1,0:T(8,128)S(1)} %get-tuple-element.37.gates_ref, bf16[512,128]{1,0:T(8,128)(2,1)S(1)} %get-tuple-element.32.query_ref, bf16[128,512]{1,0:T(8,128)(2,1)S(1)} %bitcast.11, f32[32,512]{1,0:T(8,128)S(1)} %get-tuple-element.35.rows_ref), custom_call_target="tpu_custom_call" | custom-call | flops 268435456 | bytes 2097152 | tf_op jit(solution)/shard_map/mix/pallas_call | solution.py:304
  75.2 5.8 %all-gather = bf16[1024,256]{1,0:T(8,128)(2,1)S(1)} all-gather(bf16[512,256]{1,0:T(8,128)(2,1)S(1)} %mix.1), channel_id=2, replica_groups={{0,1},{2,3},{4,5},{6,7},{8,9},{10,11},{12,13},{14,15},{16,17},{18,19},{..., dimensions={0}, use_global_device_ids=true | all-gather | bytes 786432 | tf_op jit(solution)/shard_map/all_gather | solution.py:389
  80.9 0.7 pair.1
  81.7 16.5 %all_to_all.27.pieces_ref = bf16[4,512,256]{2,1,0:T(8,128)(2,1)S(1)} all-to-all(bf16[4,512,256]{2,1,0:T(8,128)(2,1)S(1)} %pair.1), channel_id=1, replica_groups={{4,6,2,0},{5,7,3,1},{12,14,10,8},{13,15,11,9},{20,22,18,16},{21,23,19,1..., dimensions={0} | all-to-all | bytes 2097152 | tf_op jit(solution)/shard_map/all_to_all | solution.py:394
  98.2 0.8 sum.1
Async XLA Ops:
  2.2 7.3 %copy-start = (bf16[256,2048]{1,0:T(8,128)(2,1)S(1)}, bf16[256,2048]{1,0:T(8,128)(2,1)}, u32[]{:S(2)}) copy-start(bf16[256,2048]{1,0:T(8,128)(2,1)} %w_ref.1) | copy-start | bytes 3145732
  2.2 20.8 %all-to-all-start = ((bf16[4,768,256]{2,1,0:T(8,128)(2,1)}), bf16[4,768,256]{2,1,0:T(8,128)(2,1)S(1)}, u32[]{:S(2)}, u32[]{:S(2)}) async-start(bf16[4,768,256]{2,1,0:T(8,128)(2,1)} %payload.1), calls=%async_computation | async-start | bytes 3145728 | tf_op jit(solution)/shard_map/all_to_all | solution.py:334
  10.4 8.2 %collective-permute-start = (bf16[256,1024]{1,0:T(8,128)(2,1)}, bf16[256,1024]{1,0:T(8,128)(2,1)S(1)}, u32[]{:S(2)}, u32[]{:S(2)}) collective-permute-start(bf16[256,1024]{1,0:T(8,128)(2,1)} %get-tuple-element.24), channel_id=1, source_target_pairs={{0,1},{1,0},{2,3},{3,2},{4,5},{5,4},{6,7},{7,6},{8,9},{9,8},{10,11... | collective-permute-start | bytes 1572872 | tf_op jit(solution)/shard_map/ppermute | solution.py:338
  23.0 10.5 %collective-permute-start.1 = (bf16[4,768,256]{2,1,0:T(8,128)(2,1)S(1)}, bf16[4,768,256]{2,1,0:T(8,128)(2,1)S(1)}, u32[]{:S(2)}, u32[]{:S(2)}) collective-permute-start(bf16[4,768,256]{2,1,0:T(8,128)(2,1)S(1)} %all-to-all-done.a_ref), channel_id=1, source_target_pairs={{0,1},{1,0},{2,3},{3,2},{4,5},{5,4},{6,7},{7,6},{8,9},{9,8},{10,11... | collective-permute-start | bytes 4718600 | tf_op jit(solution)/shard_map/ppermute | solution.py:342
  30.4 2.1 %copy-start.1 = (bf16[2,2048,4]{1,2,0:T(4,128)(2,1)S(1)}, bf16[2,2048,4]{1,2,0:T(4,128)(2,1)}, u32[]{:S(2)}) copy-start(bf16[2,2048,4]{1,2,0:T(4,128)(2,1)} %param.11) | copy-start | bytes 98308
  32.4 1.0 %copy-start.2 = (f32[2,4]{1,0:T(2,128)S(1)}, f32[2,4]{1,0:T(2,128)}, u32[]{:S(2)}) copy-start(f32[2,4]{1,0:T(2,128)} %bias_ref.1) | copy-start | bytes 100
  32.5 1.0 %copy-start.3 = (f32[4]{0:T(128)S(1)}, f32[4]{0:T(128)}, u32[]{:S(2)}) copy-start(f32[4]{0:T(128)} %rate_ref.1) | copy-start | bytes 52
  33.5 27.9 %copy-start.4 = (f32[4]{0:T(128)S(1)}, f32[4]{0:T(128)}, u32[]{:S(2)}) copy-start(f32[4]{0:T(128)} %skip_ref.1) | copy-start | bytes 52
  36.0 9.5 %copy-start.5 = (bf16[512,256]{1,0:T(8,128)(2,1)}, bf16[512,256]{1,0:T(8,128)(2,1)S(1)}, u32[]{:S(2)}) copy-start(bf16[512,256]{1,0:T(8,128)(2,1)S(1)} %get-tuple-element.34.values_ref) | copy-start | bytes 786436
  46.3 19.4 %all-to-all-start.2 = ((bf16[8,16,384]{2,1,0:T(8,128)(2,1)}), bf16[8,16,384]{2,1,0:T(8,128)(2,1)S(1)}, u32[]{:S(2)}, u32[]{:S(2)}) async-start(bf16[8,16,384]{2,1,0:T(8,128)(2,1)} %totals.1), calls=%async_computation.2 | async-start | bytes 196608 | tf_op jit(solution)/shard_map/all_to_all | solution.py:380
  61.4 1.0 copy-start.6

commit v6 on v5

--- a/solution.py
+++ b/solution.py
@@ -16,6 +16,7 @@
 XS = 4
 GROUP = 8
 SLICE = N // GROUP
+FAR_ROWS = SLICE * (W // N) + 8
 
 X_ORDER = [2, 3, 1, 0]
 X_GROUPS = [[2 * x + c for x in X_ORDER] for c in range(2)]
@@ -25,7 +26,7 @@
 SWAP = [(i, i ^ 1) for i in range(8)]
 NEAR_ORDER = [6, 7, 5, 4, 3, 2, 1, 0]
 NEAR = [[GROUP * g + j for j in NEAR_ORDER] for g in range(8)]
-FAR_ORDER = [5, 4, 6, 7, 3, 2, 1, 0]
+FAR_ORDER = [5, 6, 4, 7, 3, 0, 2, 1]
 FAR = [[GROUP * g + j for g in FAR_ORDER] for j in range(GROUP)]
 
 VMEM = pl.BlockSpec(memory_space=pltpu.VMEM)
@@ -67,16 +68,28 @@
     return out
 
 
-def prep_kernel(tokens_ref, bc_ref, out_ref, rows_ref, sems):
+def prep_kernel(tokens_ref, bc_ref, out_ref, tokens_here, bc_here, rows_ref, in_sems, sems):
+    half = L // 2
+    reads = [pltpu.make_async_copy(bc_ref, bc_here, in_sems.at[2])]
+    for i in range(2):
+        part = pl.ds(half * i, half)
+        reads.append(pltpu.make_async_copy(tokens_ref.at[part], tokens_here.at[part], in_sems.at[i]))
+    for read in reads:
+        read.start()
     copies = []
-    for x in range(XS):
-        copies.append(pltpu.make_async_copy(tokens_ref, out_ref.at[x, pl.ds(0, L)], sems.at[x]))
-        copies[-1].start()
+
+    def spread_out(source, first):
+        for x in range(XS):
+            copies.append(pltpu.make_async_copy(source, out_ref.at[x, pl.ds(first, W)], sems.at[len(copies)]))
+            copies[-1].start()
+
+    reads[0].wait()
     for b in range(8):
-        rows_ref[32 * b : 32 * (b + 1), :] = bc_ref[:, W * b : W * (b + 1)]
-    for x in range(XS):
-        copies.append(pltpu.make_async_copy(rows_ref, out_ref.at[x, pl.ds(L, W)], sems.at[XS + x]))
-        copies[-1].start()
+        rows_ref[32 * b : 32 * (b + 1), :] = bc_here[:, W * b : W * (b + 1)]
+    spread_out(rows_ref, L)
+    for i in range(2):
+        reads[1 + i].wait()
+        spread_out(tokens_here.at[pl.ds(half * i, half)], half * i)
     for copy in copies:
         copy.wait()
 
@@ -245,25 +258,32 @@
     forward = forward.astype(BF16)
     backward = backward.astype(BF16)
     for q in range(8):
-        out_ref[q, :, 0:W] = jnp.where(FAR_ORDER[q] > g, forward, backward)
-        out_ref[q, :, W : W + N] = log
+        chosen = jnp.where(FAR_ORDER[q] > g, forward, backward)
+        for i in range(W // N):
+            out_ref[q, SLICE * i : SLICE * (i + 1), :] = chosen[:, N * i : N * (i + 1)]
+        out_ref[q, FAR_ROWS - 8 : FAR_ROWS, :] = log[0:8]
 
 
 def enter_kernel(group_ref, got_ref, far_ref, out_ref):
     g = group_ref[0]
     states, decays = near_states(got_ref)
-    extra = far_ref[:, :, W : W + N].reshape(8 * SLICE, N)
+    extra = far_ref[:, FAR_ROWS - 8 : FAR_ROWS, :].astype(F32).reshape(64, N).astype(BF16)
     decay = jnp.exp(dot(extra, spread(2 * W, 0, 4)))
+
+    def total(slot):
+        parts = [far_ref[slot, SLICE * i : SLICE * (i + 1), :] for i in range(W // N)]
+        return jnp.concatenate(parts, axis=1).astype(F32)
+
     forward = jnp.zeros((SLICE, W), F32)
     backward = jnp.zeros((SLICE, W), F32)
     for q in range(8):
         slot = FAR_ORDER.index(q)
-        rows = slice(SLICE * slot, SLICE * (slot + 1))
-        forward = jnp.where(q < g, decay[rows, :W] * forward + far_ref[slot, :, 0:W].astype(F32), forward)
+        rows = slice(8 * slot, 8 * slot + 1)
+        forward = jnp.where(q < g, decay[rows, :W] * forward + total(slot), forward)
     for q in range(7, -1, -1):
         slot = FAR_ORDER.index(q)
-        rows = slice(SLICE * slot, SLICE * (slot + 1))
-        backward = jnp.where(q > g, decay[rows, W:] * backward + far_ref[slot, :, 0:W].astype(F32), backward)
+        rows = slice(8 * slot, 8 * slot + 1)
+        backward = jnp.where(q > g, decay[rows, W:] * backward + total(slot), backward)
     for j in range(GROUP):
         out_ref[NEAR_ORDER.index(j), :, 0:W] = forward.astype(BF16)
         forward = decays[j][:, :W] * forward + states[j][:, :W]
@@ -294,10 +314,19 @@
         out_ref[SUM_ORDER.index(x)] = dot(hidden, jnp.concatenate([w_ref[:, at], other_ref[:, at]], axis=0)).astype(BF16)
 
 
-def sum_kernel(pieces_ref, out_ref):
-    total = pieces_ref[0].astype(F32) + pieces_ref[1].astype(F32)
-    total = total + pieces_ref[2].astype(F32) + pieces_ref[3].astype(F32)
-    out_ref[...] = total.astype(BF16)
+def sum_kernel(pieces_ref, out_ref, staged_ref, sems):
+    rows = L // 4
+    copies = []
+    for i in range(4):
+        at = slice(rows * i, rows * (i + 1))
+        total = pieces_ref[0, at].astype(F32) + pieces_ref[1, at].astype(F32)
+        total = total + pieces_ref[2, at].astype(F32) + pieces_ref[3, at].astype(F32)
+        staged_ref[at] = total.astype(BF16)
+        part = pl.ds(rows * i, rows)
+        copies.append(pltpu.make_async_copy(staged_ref.at[part], out_ref.at[part], sems.at[i]))
+        copies[-1].start()
+    for copy in copies:
+        copy.wait()
 
 
 def call(kernel, name, ins, outs, flops, *operands, touched=1 << 21, scratch=(), out_spec=VMEM, limit=20 << 20):
@@ -319,13 +348,19 @@
     (payload,) = call(
         prep_kernel,
         "payload",
-        [VMEM, VMEM],
+        [HBM, HBM],
         [((XS, L + W, W), BF16)],
         1,
         tokens,
         bc_weight.T,
         touched=0,
-        scratch=[pltpu.VMEM((W, W), BF16), pltpu.SemaphoreType.DMA((2 * XS,))],
+        scratch=[
+            pltpu.VMEM((L, W), BF16),
+            pltpu.VMEM((32, D), BF16),
+            pltpu.VMEM((W, W), BF16),
+            pltpu.SemaphoreType.DMA((3,)),
+            pltpu.SemaphoreType.DMA((3 * XS,)),
+        ],
         out_spec=HBM,
         limit=(64 << 20) - (64 << 10),
     )
@@ -375,7 +410,7 @@
         scratch=[pltpu.VMEM((L, N), F32)],
     )
     (totals,) = call(
-        totals_kernel, "totals", [SMEM, VMEM], [((8, SLICE, W + N), BF16)], 1 << 20, group, near
+        totals_kernel, "totals", [SMEM, VMEM], [((8, FAR_ROWS, N), BF16)], 1 << 20, group, near
     )
     far = lax.all_to_all(totals, "seq", 0, 0, axis_index_groups=FAR, tiled=True)
     far, inner = lax.optimization_barrier((far, inner))
@@ -392,7 +427,16 @@
         touched=1 << 25,
     )
     pieces = lax.all_to_all(paired, "tp", 0, 0, axis_index_groups=SUM_GROUPS, tiled=True)
-    return call(sum_kernel, "sum", [VMEM], [((L, W), BF16)], 1 << 20, pieces)[0]
+    return call(
+        sum_kernel,
+        "sum",
+        [VMEM],
+        [((L, W), BF16)],
+        1 << 20,
+        pieces,
+        scratch=[pltpu.VMEM((L, W), BF16), pltpu.SemaphoreType.DMA((4,))],
+        out_spec=HBM,
+    )[0]
 
 
 def solution(mesh):

time: 99.5 us -> 99.1 us (level)
  no operation moved by 1% of the time
where the time goes in v6:
time: 99.1 us; the launch traced here: 98.6 us
  blocking collectives  40.2 us (41%)
  starting transfers between devices  36.1 us (36%)
  Pallas kernels  12.4 us (13%)
  waiting for transfers between devices  6.72 us (7%)
  local copies, waits for them, and re-layouts  3.03 us (3%)
    all_to_all x1, blocking collectives, shards(): lax.all_to_all(paired, 'tp', 0, 0, axis_index_groups=SUM_GROUPS, tiled=True)  16.5 us
    all_to_all x1, starting transfers between devices, shards(): far = lax.all_to_all(totals, 'seq', 0, 0, axis_index_groups=FAR, tiled=True)  15 us
    pallas_call x10, Pallas kernels, call(): pl.pallas_call(kernel, name=name, in_specs=ins, out_specs=[out_spec] * le...  12.4 us
    all_to_all x1, blocking collectives, shards(): lax.all_to_all(message, 'seq', 0, 0, axis_index_groups=NEAR, tiled=True)  9.48 us
    all_to_all x1, blocking collectives, shards(): lax.all_to_all(enters, 'seq', 0, 0, axis_index_groups=NEAR, tiled=True)  8.75 us
    ppermute x1, starting transfers between devices, shards(): theirs = lax.ppermute(mine, 'tp', SWAP)  7.38 us
    all_to_all x1, starting transfers between devices, shards(): lax.all_to_all(payload, 'tp', 0, 0, axis_index_groups=X_GROUPS, tiled=True)  7.25 us
    ppermute x1, starting transfers between devices, shards(): other_weight = lax.ppermute(other_weight, 'tp', SWAP)  6.46 us
  transfers between devices with their start and end apart: 4, of which 3 were waited for; matrix products, arithmetic and copies ran while one was open for 2% of the time, Pallas kernels for 4%

profile of v6, /device:TPU:1, one launch (start us, length us, event | category | flops | bytes accessed | tf_op | source)
XLA Modules:
  0.0 98.6 jit_solution(10007179754874212428)
XLA Ops:
  0.0 2.2 %payload.1 = bf16[4,768,256]{2,1,0:T(8,128)(2,1)} custom-call(bf16[512,256]{1,0:T(8,128)(2,1)} %tokens_ref.1, bf16[32,2048]{1,0:T(8,128)(2,1)} %bitcast.14), custom_call_target="tpu_custom_call" | custom-call | flops 1 | tf_op jit(solution)/shard_map/payload/pallas_call | solution.py:333
  2.2 0.0 copy-start
  2.2 7.3 %all-to-all-start = ((bf16[4,768,256]{2,1,0:T(8,128)(2,1)}), bf16[4,768,256]{2,1,0:T(8,128)(2,1)S(1)}, u32[]{:S(2)}, u32[]{:S(2)}) async-start(bf16[4,768,256]{2,1,0:T(8,128)(2,1)} %payload.1), calls=%async_computation | async-start | bytes 3145728 | tf_op jit(solution)/shard_map/all_to_all | solution.py:369
  9.5 0.0 copy-done
  9.5 1.0 columns.1
  10.4 6.5 %collective-permute-start = (bf16[256,1024]{1,0:T(8,128)(2,1)}, bf16[256,1024]{1,0:T(8,128)(2,1)S(1)}, u32[]{:S(2)}, u32[]{:S(2)}) collective-permute-start(bf16[256,1024]{1,0:T(8,128)(2,1)} %get-tuple-element.24), channel_id=1, source_target_pairs={{0,1},{1,0},{2,3},{3,2},{4,5},{5,4},{6,7},{7,6},{8,9},{9,8},{10,11... | collective-permute-start | bytes 1572872 | tf_op jit(solution)/shard_map/ppermute | solution.py:373
  16.9 1.7 %collective-permute-done.other_ref = bf16[256,1024]{1,0:T(8,128)(2,1)S(1)} collective-permute-done((bf16[256,1024]{1,0:T(8,128)(2,1)}, bf16[256,1024]{1,0:T(8,128)(2,1)S(1)}, u32[]{:S(2)}, u32[]{:S(2)}) %collective-permute-start) | collective-permute-done | bytes 524320 | tf_op jit(solution)/shard_map/ppermute | solution.py:373
  18.6 4.3 %all-to-all-done.a_ref = bf16[4,768,256]{2,1,0:T(8,128)(2,1)S(1)} async-done(((bf16[4,768,256]{2,1,0:T(8,128)(2,1)}), bf16[4,768,256]{2,1,0:T(8,128)(2,1)S(1)}, u32[]{:S(2)}, u32[]{:S(2)}) %all-to-all-start) | async-done | bytes 1572896 | tf_op jit(solution)/shard_map/all_to_all | solution.py:369
  23.0 7.4 %collective-permute-start.1 = (bf16[4,768,256]{2,1,0:T(8,128)(2,1)S(1)}, bf16[4,768,256]{2,1,0:T(8,128)(2,1)S(1)}, u32[]{:S(2)}, u32[]{:S(2)}) collective-permute-start(bf16[4,768,256]{2,1,0:T(8,128)(2,1)S(1)} %all-to-all-done.a_ref), channel_id=1, source_target_pairs={{0,1},{1,0},{2,3},{3,2},{4,5},{5,4},{6,7},{7,6},{8,9},{9,8},{10,11... | collective-permute-start | bytes 4718600 | tf_op jit(solution)/shard_map/ppermute | solution.py:377
  30.3 0.0 copy-start.1
  30.4 2.0 %copy.9 = bf16[256,8,2,256]{3,1,2,0:T(8,128)(2,1)S(1)} copy(bf16[256,8,2,256]{3,2,1,0:T(2,128)(2,1)} %bitcast.13) | data formatting | bytes 4194304
  32.4 0.0 copy-done.1
  32.4 0.0 copy-start.2
  32.4 0.0 copy-start.3
  32.4 1.0 %half.1 = (f32[512,512]{1,0:T(8,128)S(1)}, f32[144,512]{1,0:T(8,128)S(1)}, bf16[16,2048]{1,0:T(8,128)(2,1)S(1)}) custom-call(s32[1]{0:T(128)} %bitcast.1.core_ref, bf16[4,768,256]{2,1,0:T(8,128)(2,1)S(1)} %all-to-all-done.a_ref, bf16[2048,512]{1,0:T(8,128)(2,1)S(1)} %bitcast.8, bf16[2,4,2048]{2,1,0:T(4,128)(2,1)S(1)} %bitcast.12), custom_call_target="tpu_custom_call" | custom-call | flops 1073741824 | bytes 2097152 | tf_op jit(solution)/shard_map/half/pallas_call | solution.py:333
  33.5 0.0 collective-permute-done.1.b_ref
  33.5 0.0 copy-done.2
  33.5 0.0 copy-done.3
  33.5 0.0 copy-start.4
  33.5 2.4 %project.1 = (bf16[512,256]{1,0:T(8,128)(2,1)S(1)}, f32[512,256]{1,0:T(8,128)S(1)}, bf16[512,128]{1,0:T(8,128)(2,1)S(1)}, bf16[128,512]{1,0:T(8,128)(2,1)S(1)}, ...) custom-call(s32[1]{0:T(128)} %bitcast.1.core_ref, f32[2,4]{1,0:T(2,128)S(1)} %copy-done.2, f32[4]{0:T(128)S(1)} %copy-done.3, ...), custom_call_target="tpu_custom_call" | custom-call | flops 2147483648 | bytes 2097152 | tf_op jit(solution)/shard_map/project/pallas_call | solution.py:333
  35.9 0.0 copy-start.5
  36.0 9.5 %all_to_all.25.got_ref = bf16[8,16,640]{2,1,0:T(8,128)(2,1)S(1)} all-to-all(bf16[8,16,640]{2,1,0:T(8,128)(2,1)S(1)} %get-tuple-element.31), channel_id=1, replica_groups={{48,56,40,32,24,16,8,0},{112,120,104,96,88,80,72,64},{176,184,168,160,1..., dimensions={0} | all-to-all | bytes 327680 | tf_op jit(solution)/shard_map/all_to_all | solution.py:402
  45.4 0.0 copy-done.5
  45.4 0.8 totals.1
  46.3 15.0 %all-to-all-start.2 = ((bf16[8,40,128]{2,1,0:T(8,128)(2,1)}), bf16[8,40,128]{2,1,0:T(8,128)(2,1)S(1)}, u32[]{:S(2)}, u32[]{:S(2)}) async-start(bf16[8,40,128]{2,1,0:T(8,128)(2,1)} %totals.1), calls=%async_computation.2 | async-start | bytes 163840 | tf_op jit(solution)/shard_map/all_to_all | solution.py:415
  61.3 0.0 copy-done.4
  61.3 0.0 copy-start.6
  61.3 0.9 copy-done.6
  62.3 2.2 %inside.1.inner_ref = f32[512,256]{1,0:T(8,128)S(1)} custom-call(f32[4]{0:T(128)S(1)} %copy-done.4, bf16[512,128]{1,0:T(8,128)(2,1)S(1)} %get-tuple-element.32.query_ref, bf16[128,512]{1,0:T(8,128)(2,1)S(1)} %get-tuple-element.33.key_ref, bf16[512,256]{1,0:T(8,128)(2,1)S(1)} %copy-done.6, f32[32,512]{1,0:T(8,128)S(1)} %get-tuple-element.35.rows_ref), custom_call_target="tpu_custom_call" | custom-call | flops 2147483648 | bytes 2097152 | tf_op jit(solution)/shard_map/inside/pallas_call | solution.py:333
  64.4 0.7 all-to-all-done.2.far_ref
  65.1 0.3 enters.1
  65.4 8.7 %all_to_all.26 = bf16[8,16,512]{2,1,0:T(8,128)(2,1)S(1)} all-to-all(bf16[8,16,512]{2,1,0:T(8,128)(2,1)S(1)} %enters.1), channel_id=1, replica_groups={{48,56,40,32,24,16,8,0},{112,120,104,96,88,80,72,64},{176,184,168,160,1..., dimensions={0} | all-to-all | bytes 262144 | tf_op jit(solution)/shard_map/all_to_all | solution.py:420
  74.1 1.0 %mix.1 = bf16[512,256]{1,0:T(8,128)(2,1)S(1)} custom-call(f32[512,256]{1,0:T(8,128)S(1)} %inside.1.inner_ref, f32[512,256]{1,0:T(8,128)S(1)} %get-tuple-element.37.gates_ref, bf16[512,128]{1,0:T(8,128)(2,1)S(1)} %get-tuple-element.32.query_ref, bf16[128,512]{1,0:T(8,128)(2,1)S(1)} %bitcast.11, f32[32,512]{1,0:T(8,128)S(1)} %get-tuple-element.35.rows_ref), custom_call_target="tpu_custom_call" | custom-call | flops 268435456 | bytes 2097152 | tf_op jit(solution)/shard_map/mix/pallas_call | solution.py:333
  75.1 5.4 %all-gather = bf16[1024,256]{1,0:T(8,128)(2,1)S(1)} all-gather(bf16[512,256]{1,0:T(8,128)(2,1)S(1)} %mix.1), channel_id=2, replica_groups={{0,1},{2,3},{4,5},{6,7},{8,9},{10,11},{12,13},{14,15},{16,17},{18,19},{..., dimensions={0}, use_global_device_ids=true | all-gather | bytes 786432 | tf_op jit(solution)/shard_map/all_gather | solution.py:424
  80.5 0.7 pair.1
  81.2 16.5 %all_to_all.27.pieces_ref = bf16[4,512,256]{2,1,0:T(8,128)(2,1)S(1)} all-to-all(bf16[4,512,256]{2,1,0:T(8,128)(2,1)S(1)} %pair.1), channel_id=1, replica_groups={{4,6,2,0},{5,7,3,1},{12,14,10,8},{13,15,11,9},{20,22,18,16},{21,23,19,1..., dimensions={0} | all-to-all | bytes 2097152 | tf_op jit(solution)/shard_map/all_to_all | solution.py:429
  97.8 0.8 sum.1
Async XLA Ops:
  2.2 7.3 %copy-start = (bf16[256,2048]{1,0:T(8,128)(2,1)S(1)}, bf16[256,2048]{1,0:T(8,128)(2,1)}, u32[]{:S(2)}) copy-start(bf16[256,2048]{1,0:T(8,128)(2,1)} %w_ref.1) | copy-start | bytes 3145732
  2.2 20.8 %all-to-all-start = ((bf16[4,768,256]{2,1,0:T(8,128)(2,1)}), bf16[4,768,256]{2,1,0:T(8,128)(2,1)S(1)}, u32[]{:S(2)}, u32[]{:S(2)}) async-start(bf16[4,768,256]{2,1,0:T(8,128)(2,1)} %payload.1), calls=%async_computation | async-start | bytes 3145728 | tf_op jit(solution)/shard_map/all_to_all | solution.py:369
  10.4 8.2 %collective-permute-start = (bf16[256,1024]{1,0:T(8,128)(2,1)}, bf16[256,1024]{1,0:T(8,128)(2,1)S(1)}, u32[]{:S(2)}, u32[]{:S(2)}) collective-permute-start(bf16[256,1024]{1,0:T(8,128)(2,1)} %get-tuple-element.24), channel_id=1, source_target_pairs={{0,1},{1,0},{2,3},{3,2},{4,5},{5,4},{6,7},{7,6},{8,9},{9,8},{10,11... | collective-permute-start | bytes 1572872 | tf_op jit(solution)/shard_map/ppermute | solution.py:373
  23.0 10.5 %collective-permute-start.1 = (bf16[4,768,256]{2,1,0:T(8,128)(2,1)S(1)}, bf16[4,768,256]{2,1,0:T(8,128)(2,1)S(1)}, u32[]{:S(2)}, u32[]{:S(2)}) collective-permute-start(bf16[4,768,256]{2,1,0:T(8,128)(2,1)S(1)} %all-to-all-done.a_ref), channel_id=1, source_target_pairs={{0,1},{1,0},{2,3},{3,2},{4,5},{5,4},{6,7},{7,6},{8,9},{9,8},{10,11... | collective-permute-start | bytes 4718600 | tf_op jit(solution)/shard_map/ppermute | solution.py:377
  30.3 2.1 %copy-start.1 = (bf16[2,2048,4]{1,2,0:T(4,128)(2,1)S(1)}, bf16[2,2048,4]{1,2,0:T(4,128)(2,1)}, u32[]{:S(2)}) copy-start(bf16[2,2048,4]{1,2,0:T(4,128)(2,1)} %param.11) | copy-start | bytes 98308
  32.4 1.0 %copy-start.2 = (f32[2,4]{1,0:T(2,128)S(1)}, f32[2,4]{1,0:T(2,128)}, u32[]{:S(2)}) copy-start(f32[2,4]{1,0:T(2,128)} %bias_ref.1) | copy-start | bytes 100
  32.4 1.0 %copy-start.3 = (f32[4]{0:T(128)S(1)}, f32[4]{0:T(128)}, u32[]{:S(2)}) copy-start(f32[4]{0:T(128)} %rate_ref.1) | copy-start | bytes 52
  33.5 27.8 %copy-start.4 = (f32[4]{0:T(128)S(1)}, f32[4]{0:T(128)}, u32[]{:S(2)}) copy-start(f32[4]{0:T(128)} %skip_ref.1) | copy-start | bytes 52
  35.9 9.5 %copy-start.5 = (bf16[512,256]{1,0:T(8,128)(2,1)}, bf16[512,256]{1,0:T(8,128)(2,1)S(1)}, u32[]{:S(2)}) copy-start(bf16[512,256]{1,0:T(8,128)(2,1)S(1)} %get-tuple-element.34.values_ref) | copy-start | bytes 786436
  46.3 18.8 %all-to-all-start.2 = ((bf16[8,40,128]{2,1,0:T(8,128)(2,1)}), bf16[8,40,128]{2,1,0:T(8,128)(2,1)S(1)}, u32[]{:S(2)}, u32[]{:S(2)}) async-start(bf16[8,40,128]{2,1,0:T(8,128)(2,1)} %totals.1), calls=%async_computation.2 | async-start | bytes 163840 | tf_op jit(solution)/shard_map/all_to_all | solution.py:415
  61.3 1.0 copy-start.6
